TPU v7x, 32 devices: a whole 2x2x4 slice. The times are simulated.
32 devices in a mesh: tm: 4 (over x, core), tile: 8 (over z, y).
Axes of the slice: x: 2, y: 2, z: 4, core: 2. Of those that a mesh axis runs over, the one named last changes fastest.
Arguments:
- recording: bfloat16 [65536, 512], P('tile', 'tm'), may hold values from -300 to 300
- footprints: bfloat16 [65536, 256], P('tile'), may hold values from -0.375 to 0.375
- pattern: int32 [256, 4], P('tile'), may hold values from 0 to 35, as said below
- decay: float32 [16384], P('tile'), may hold values from 0.96 to 1
- frame_gain: float32 [512], P('tm'), may hold values from 0.6 to 1
- spikes: float32 [16384, 512], P('tile', 'tm'), may hold values from 0 to 0.15
Outputs:
- spikes_out: float32 [16384, 512], P('tile', 'tm')
- traces_last: float32 [16384, 512], P('tile', 'tm')
Inputs may be any that keep to these rules, and one draw needn't show every extreme that they name: `pattern`: with p = q % 32, row q holds 4 different values between p and p + 4, always including p, p + 2 and p + 4, in some order; value v names the stripe's own neuron block v - 2, so values under 2 or over 2048 // 64 + 1 name edge blocks of the adjacent stripes.
All inputs are finite; a program needn't handle non-finite values.
Results may differ from a plain program's by a relative error of at most 0.00073.
Values may be sent and summed in bfloat16 or wider, within the bound.
No kernel may reach another device: no remote copies, remote signals or barrier semaphores. Data moves between devices by JAX's collectives and lax.ppermute only.
A program may use at most 128 MiB of HBM per device.

v0:
```python
import jax
import jax.numpy as jnp
from jax import lax
from jax.experimental import pallas as pl
from jax.experimental.pallas import tpu as pltpu
from jax.sharding import PartitionSpec as P

NEU_BLOCK = 64
PIX_BLOCK = 256
PARTS = 4
K = 4
HB = 2
ITERS = 2
LANES = 128
RIM = HB * NEU_BLOCK // LANES
F32 = jnp.float32
BF16 = jnp.bfloat16
VMEM = pl.BlockSpec(memory_space=pltpu.VMEM)
HBM = pl.BlockSpec(memory_space=pltpu.HBM)
SMEM = pl.BlockSpec(memory_space=pltpu.SMEM)


def padded8(rows):
    return -(-rows // 8) * 8


def table(frames, reverse):
    row = lax.broadcasted_iota(jnp.int32, (frames, 2 * frames), 0)
    col = lax.broadcasted_iota(jnp.int32, (frames, 2 * frames), 1)
    col = jnp.where(col >= frames, col - frames, col)
    keep = col >= row if reverse else col <= row
    return jnp.where(keep, 1.0, 0.0).astype(BF16)


def summed(sums_table, values):
    high = values.astype(BF16)
    low = (values - high.astype(F32)).astype(BF16)
    both = jnp.concatenate([high, low], axis=0)
    return jnp.dot(sums_table, both, preferred_element_type=F32)


def powers(log_decay, frames, mid, sign):
    groups = frames // 8
    coarse = (8 * lax.broadcasted_iota(jnp.int32, (groups, LANES), 0) - mid).astype(F32) * sign
    fine = lax.broadcasted_iota(jnp.int32, (8, LANES), 0).astype(F32) * sign
    coarse = jnp.exp(coarse * log_decay)
    fine = jnp.exp(fine * log_decay)
    return (coarse[:, None, :] * fine[None, :, :]).reshape(frames, LANES)


def chunk(field, c):
    own, rim = field
    inner = own.shape[0]
    if c < RIM:
        return rim.at[c]
    if c >= RIM + inner:
        return rim.at[c - inner]
    return own.at[c - RIM]


def chunk_count(field):
    return field[0].shape[0] + field[1].shape[0]


def prep_chunk(c, rate, field, gains, s3, p3, pinv3, z3, rows, pay):
    frames = field.shape[1]
    middle, prefix_col, inverse_col, sums_table = gains
    mid = frames // 2 - 1
    rate = jnp.where(rate > 0.0, rate, 1.0)
    log_rate = jnp.log(rate)
    gain = jnp.sqrt(1.0 - rate * rate)
    p = powers(log_rate, frames, mid, 1.0) * prefix_col
    pinv = powers(log_rate, frames, mid, -1.0) * inverse_col
    field = field.T
    z = summed(sums_table, field * gain * pinv)
    last = p[frames - 1 : frames, :]
    s3[...] = field
    p3[...] = p
    pinv3[...] = pinv
    z3[...] = z
    half = rate
    for _ in range(frames.bit_length() - 2):
        half = half * half
    rows[0, c : c + 1, :] = gain
    rows[1, c : c + 1, :] = half * middle
    rows[2, c : c + 1, :] = half * half
    pay[0, c : c + 1, :] = last * z[frames - 1 : frames, :]
    scale = last * gain
    pay[1, c : c + 1, :] = scale * scale * jnp.sum(pinv * pinv, axis=0, keepdims=True)


def gain_columns(gains):
    frames = gains.shape[1]
    mid = frames // 2 - 1
    lane = lax.broadcasted_iota(jnp.int32, (8, frames), 1)
    prefix = jnp.broadcast_to(gains, (8, frames))
    step = 1
    while step < frames:
        prefix = prefix * jnp.where(lane >= step, pltpu.roll(prefix, step, 1), 1.0)
        step *= 2
    middle = jnp.broadcast_to(prefix[0:1, mid : mid + 1], (1, LANES))
    whole = jnp.broadcast_to(prefix[0:1, frames - 1 : frames], (1, LANES))
    prefix_col = jnp.broadcast_to(prefix[0:1] / middle, (LANES, frames)).T
    inverse_col = jnp.broadcast_to(middle / prefix[0:1], (LANES, frames)).T
    return middle, whole, prefix_col, inverse_col


def rims_kernel(spikes, decay, gains, first, second, rates_here, gains_here, sems):
    edge = RIM * LANES
    neurons = spikes.shape[0]
    own = decay.shape[0]
    even = lax.axis_index("tile") % 2 == 0
    top = jnp.where(even, neurons - edge, 0)
    bottom = jnp.where(even, 0, neurons - edge)
    copies = [
        pltpu.make_async_copy(decay, rates_here, sems.at[0]),
        pltpu.make_async_copy(gains, gains_here, sems.at[1]),
        pltpu.make_async_copy(
            spikes.at[pl.ds(pl.multiple_of(top, LANES), edge)], first.at[pl.ds(0, edge)], sems.at[2]
        ),
        pltpu.make_async_copy(
            spikes.at[pl.ds(pl.multiple_of(bottom, LANES), edge)],
            second.at[pl.ds(0, edge)],
            sems.at[3],
        ),
    ]
    for copy in copies:
        copy.start()
    first[edge:, :] = jnp.zeros_like(first[edge:, :])
    second[edge:, :] = jnp.zeros_like(second[edge:, :])
    copies[0].wait()
    lower, upper = rates_here[0:RIM, :], rates_here[own - RIM : own, :]
    first[edge : edge + RIM, :] = jnp.where(even, upper, lower)
    second[edge : edge + RIM, :] = jnp.where(even, lower, upper)
    for copy in copies[1:]:
        copy.wait()


def prep_own_kernel(
    spikes, decay, gains, feet, s3, p3, pinv3, z3, rows, pay, columns, feet_here, spikes_here, sems
):
    own = s3.shape[0]
    chunks = own + 2 * RIM
    size = spikes.shape[0] // PARTS
    copies = [
        pltpu.make_async_copy(
            spikes.at[pl.ds(i * size, size)], spikes_here.at[pl.ds(i * size, size)], sems.at[i]
        )
        for i in range(PARTS)
    ]
    for copy in copies:
        copy.start()
    fetch = pltpu.make_async_copy(feet, feet_here, sems.at[PARTS])
    fetch.start()
    middle, whole, prefix_col, inverse_col = gain_columns(gains[...])
    columns[0] = prefix_col
    columns[1] = inverse_col
    rows[...] = jnp.ones_like(rows)
    rows[0, chunks : chunks + 1, :] = middle
    pay[...] = jnp.zeros_like(pay)
    pay[0, chunks : chunks + 1, :] = whole
    shared = middle, prefix_col, inverse_col, table(spikes.shape[1], False)
    for i in range(own):
        if i % (own // PARTS) == 0:
            copies[i // (own // PARTS)].wait()
        field = spikes_here[i * LANES : (i + 1) * LANES, :]
        at = [ref.at[i] for ref in (s3, p3, pinv3, z3)]
        prep_chunk(i + RIM, decay[i : i + 1, :], field, shared, *at, rows, pay)
    fetch.wait()


def sides(even, first, second):
    return jnp.where(even, second, first), jnp.where(even, first, second)


def prep_rim_kernel(first, second, columns, rows_own, pay_own, s3, p3, pinv3, z3, rows, pay):
    rims, frames = s3.shape[0], s3.shape[1]
    own = rows_own.shape[1] - padded8(1)
    chunks = own + 2 * RIM
    middle = rows_own[0, chunks : chunks + 1, :]
    shared = middle, columns[0], columns[1], table(frames, False)
    rows[...] = rows_own[...]
    pay[...] = pay_own[...]
    even = lax.axis_index("tile") % 2 == 0
    below, above = sides(even, first[...], second[...])
    for i in range(rims):
        message = below if i < RIM else above
        j = i % RIM
        c = i if i < RIM else own + i
        at = [ref.at[i] for ref in (s3, p3, pinv3, z3)]
        field = message[j * LANES : (j + 1) * LANES, :]
        rate = message[RIM * LANES + j : RIM * LANES + j + 1, :]
        prep_chunk(c, rate, field, shared, *at, rows, pay)


def block_totals(pays, chunks, rows):
    return [rows[2] * pays[m, 0, chunks : chunks + 1, :] for m in range(pays.shape[0])]


def step_size(stats):
    both = jnp.sum(jnp.sum(stats[...], axis=0), axis=1, keepdims=True)
    return jnp.broadcast_to(both[0:1] / (both[1:2] + 1e-06), (1, LANES))


def update_kernel(s3, g3, stats, p3, pinv3, rows, new3, z3, pay):
    chunks = chunk_count(s3)
    frames = g3.shape[1]
    sums_table = table(frames, False)
    size = step_size(stats)
    pay[...] = jnp.zeros_like(pay)
    for c in range(chunks):
        field = jnp.maximum(chunk(s3, c)[...] - size * g3[c], 0.0)
        z = summed(sums_table, field * rows[0, c : c + 1, :] * chunk(pinv3, c)[...])
        if len(new3) == 2:
            chunk(new3, c)[...] = field
        elif RIM <= c < chunks - RIM:
            new3[0][c - RIM] = field
        chunk(z3, c)[...] = z
        last = chunk(p3, c)[frames - 1 : frames, :]
        pay[c : c + 1, :] = last * z[frames - 1 : frames, :]


def final_kernel(s3, g3, stats, out, here, sems):
    size = step_size(stats)
    own = s3.shape[0]
    rows = out.shape[0] // PARTS
    copies = [
        pltpu.make_async_copy(
            here.at[pl.ds(i * rows, rows)], out.at[pl.ds(i * rows, rows)], sems.at[i]
        )
        for i in range(PARTS)
    ]
    for i in range(own):
        field = jnp.maximum(s3[i] - size * g3[i + RIM], 0.0)
        here[i * LANES : (i + 1) * LANES, :] = field.T
        if (i + 1) % (own // PARTS) == 0:
            copies[i // (own // PARTS)].start()
    for copy in copies:
        copy.wait()


def picked(ext, pattern, q):
    parts = [
        ext[pl.ds(pl.multiple_of(pattern[k, q] * NEU_BLOCK, NEU_BLOCK), NEU_BLOCK), :]
        for k in range(K)
    ]
    return jnp.concatenate(parts, axis=0)


def foot_of(feet, q):
    return feet[q * PIX_BLOCK : (q + 1) * PIX_BLOCK, :]


def pull_back(pattern, ext, feet, record, contrib, place, start, stop):
    for q in range(start, stop):
        for v in range(2 * HB + 1):
            place[q, v] = -1
        for k in range(K):
            place[q, pattern[k, q] - q] = k
    for q in range(start, stop):
        foot = foot_of(feet, q)
        fitted = jnp.dot(foot, picked(ext, pattern, q), preferred_element_type=F32)
        residual = (fitted - foot_of(record, q).astype(F32)).astype(BF16)
        contrib[q * K * NEU_BLOCK : (q + 1) * K * NEU_BLOCK, :] = lax.dot_general(
            foot, residual, (((0,), (0,)), ((), ())), preferred_element_type=F32
        )


def gathered(contrib, place, c, ranges):
    frames = contrib.shape[1]
    per_chunk = LANES // NEU_BLOCK
    halves = []
    for b in range(c * per_chunk, (c + 1) * per_chunk):
        total = jnp.zeros((NEU_BLOCK, frames), F32)
        for v in range(2 * HB + 1):
            q = b - v
            if any(start <= q < stop for start, stop in ranges):
                k = place[q, v]
                at = pl.multiple_of((q * K + jnp.maximum(k, 0)) * NEU_BLOCK, NEU_BLOCK)
                value = contrib[pl.ds(at, NEU_BLOCK), :]
                if v % 2:
                    value = jnp.where(k >= 0, value, 0.0)
                total = total + value
        halves.append(total)
    return jnp.concatenate(halves, axis=0).T


def edge_kernel(
    pattern, z3, p3, rows, pay, pays, feet, record, ext, zones, spill, send_a, send_b, state, *scratch
):
    contrib, place = scratch
    chunks = chunk_count(z3)
    stripe = pattern.shape[1]
    edge = 2 * HB
    me = lax.axis_index("tm")
    totals = block_totals(pay, chunks, rows)
    carry = jnp.zeros_like(totals[0])
    for m in range(pays.shape[0]):
        carry = jnp.where(m < me, pays[m] + totals[m] * carry, carry)
    carry = carry * rows[1]
    state[...] = carry
    for c in range(chunks):
        field = chunk(p3, c)[...] * (chunk(z3, c)[...] + carry[c : c + 1, :])
        ext[c * LANES : (c + 1) * LANES, :] = field.T.astype(BF16)
    ranges = ((0, edge), (stripe - edge, stripe))
    for start, stop in ranges:
        pull_back(pattern, ext, feet, record, contrib, place, start, stop)
    even = lax.axis_index("tile") % 2 == 0
    for i in range(2 * RIM):
        below = gathered(contrib, place, i, ranges)
        above = gathered(contrib, place, chunks - 2 * RIM + i, ranges)
        zones[i] = below
        zones[2 * RIM + i] = above
        send_a[i] = jnp.where(even, above, below).astype(BF16)
        send_b[i] = jnp.where(even, below, above).astype(BF16)
        spill[i] = gathered(contrib, place, 2 * RIM + i, ranges)
        spill[2 * RIM + i] = gathered(contrib, place, chunks - 4 * RIM + i, ranges)


def adjoint_chunk(sums_table, field, p, pinv, rows, c, r3, pay):
    frames = field.shape[0]
    r = summed(sums_table, field * p)
    r3[...] = r
    gain = rows[0, c : c + 1, :]
    pay[0, c : c + 1, :] = rows[1, c : c + 1, :] * r[0:1, :]
    ends = p[frames - 1 : frames, :] * gain * gain
    pay[1, c : c + 1, :] = ends * jnp.sum(pinv * pinv * r, axis=0, keepdims=True)


def inner_kernel(pattern, p3, pinv3, rows, ext, spill, feet, record, r3, pay, *scratch):
    contrib, place = scratch
    chunks = chunk_count(p3)
    frames = spill.shape[1]
    stripe = pattern.shape[1]
    edge = 2 * HB
    pull_back(pattern, ext, feet, record, contrib, place, edge, stripe - edge)
    sums_table = table(frames, True)
    pay[...] = jnp.zeros_like(pay)
    inner = chunks - 4 * RIM
    for i in range(inner):
        c = i + 2 * RIM
        field = gathered(contrib, place, c, ((edge, stripe - edge),))
        if i < 2 * RIM:
            field = field + spill[i]
        if i >= inner - 2 * RIM:
            field = field + spill[i - inner + 4 * RIM]
        p, pinv = chunk(p3, c)[...], chunk(pinv3, c)[...]
        adjoint_chunk(sums_table, field, p, pinv, rows, c, r3.at[i], pay)


def border_kernel(zones, got_a, got_b, p3, pinv3, rows, pay_inner, r3, pay):
    chunks = chunk_count(p3)
    frames = zones.shape[1]
    sums_table = table(frames, True)
    pay[...] = pay_inner[...]
    even = lax.axis_index("tile") % 2 == 0
    for i in range(2 * RIM):
        both = sides(even, got_a[i].astype(F32), got_b[i].astype(F32))
        for side, c in ((0, i), (1, chunks - 2 * RIM + i)):
            at = side * 2 * RIM + i
            field = zones[at] + both[side]
            p, pinv = chunk(p3, c)[...], chunk(pinv3, c)[...]
            adjoint_chunk(sums_table, field, p, pinv, rows, c, r3.at[at], pay)


def direction_kernel(
    pattern, r_inner, r_border, p3, pinv3, rows, pay, pays, feet, g3, stats, ext
):
    chunks, frames = g3.shape[0], g3.shape[1]
    own = chunks - 2 * RIM
    stripe = pattern.shape[1]
    me = lax.axis_index("tm")
    totals = block_totals(pay, chunks, rows)
    blocks = pays.shape[0]
    entering = [None] * blocks
    state = jnp.zeros_like(totals[0])
    for m in reversed(range(blocks)):
        entering[m] = state
        state = pays[m, 0] + totals[m] * state
    carry = jnp.zeros_like(totals[0])
    adjoint = jnp.zeros_like(totals[0])
    for m in range(blocks):
        end = pays[m, 1] + pay[m, 1] * entering[m]
        carry = jnp.where(m < me, end + totals[m] * carry, carry)
        adjoint = jnp.where(m == me, entering[m], adjoint)
    carry = carry * rows[1]
    sums_table = table(frames, False)
    grad_sq = jnp.zeros((8, LANES), F32)
    for c in range(chunks):
        p, pinv = chunk(p3, c)[...], chunk(pinv3, c)[...]
        if c < 2 * RIM:
            r = r_border[c]
        elif c >= chunks - 2 * RIM:
            r = r_border[c - chunks + 4 * RIM]
        else:
            r = r_inner[c - 2 * RIM]
        gain = rows[0, c : c + 1, :]
        gradient = gain * pinv * (r + p[frames - 1 : frames, :] * adjoint[c : c + 1, :])
        g3[c] = gradient
        if RIM <= c < RIM + own:
            grad_sq += jnp.sum((gradient * gradient).reshape(frames // 8, 8, LANES), axis=0)
        z = summed(sums_table, gain * gradient * pinv)
        field = (p * (z + carry[c : c + 1, :])).T
        ext[c * LANES : (c + 1) * LANES, :] = field.astype(BF16)
    image_sq = jnp.zeros((8, frames), F32)
    for q in range(stripe):
        image = jnp.dot(foot_of(feet, q), picked(ext, pattern, q), preferred_element_type=F32)
        image_sq += jnp.sum((image * image).reshape(PIX_BLOCK // 8, 8, frames), axis=0)
    both = jnp.concatenate(
        [
            jnp.sum(grad_sq, axis=0, keepdims=True),
            jnp.sum(image_sq, axis=0, keepdims=True),
        ],
        axis=0,
    )
    stats[...] = jnp.broadcast_to(both[None], stats.shape)


def traces_kernel(z3, p3, state, traces):
    for i in range(z3.shape[0]):
        c = i + RIM
        field = p3[i] * (z3[i] + state[c : c + 1, :])
        traces[i * LANES : (i + 1) * LANES, :] = field.T


def f32(*shape):
    return jax.ShapeDtypeStruct(shape, F32)


def bf16(*shape):
    return jax.ShapeDtypeStruct(shape, BF16)


def call(
    kernel, name, micros, outs, args, scratch=(), far=(), far_out=False, keep=(), limit=16
):
    def spec(place, arg):
        if place in far:
            return HBM
        return SMEM if arg.dtype == jnp.int32 else VMEM

    in_specs = [jax.tree.map(lambda x: spec(i, x), arg) for i, arg in enumerate(args)]
    in_specs.append(jax.tree.map(lambda _: VMEM, keep))

    def body(*refs):
        kernel(*refs[: len(args)], *refs[len(args) + 1 :])

    return pl.pallas_call(
        body,
        name=name,
        out_shape=outs,
        in_specs=in_specs,
        out_specs=jax.tree.map(lambda _: HBM if far_out else VMEM, outs),
        scratch_shapes=scratch,
        compiler_params=pltpu.CompilerParams(vmem_limit_bytes=int(limit * 2**20)),
        cost_estimate=pl.CostEstimate(
            flops=int(micros * 1e8), bytes_accessed=int(micros * 3e6), transcendentals=0
        ),
    )(*args, keep)


def swapped(first, second):
    size = lax.axis_size("tile")

    def pairs(start):
        both = [(i, i + 1) for i in range(start, size - 1, 2)]
        return both + [(j, i) for i, j in both]

    return lax.ppermute(first, "tile", pairs(0)), lax.ppermute(second, "tile", pairs(1))


def per_device(recording, footprints, pattern, decay, frame_gain, spikes):
    neurons, frames = spikes.shape
    stripe = pattern.shape[0]
    pattern = pattern.T
    own = neurons // LANES
    chunks = own + 2 * RIM
    lines = own + padded8(1)
    devices = lax.axis_size("tile") * lax.axis_size("tm")
    split = (f32(own, frames, LANES), f32(2 * RIM, frames, LANES))
    message = f32(RIM * LANES + padded8(RIM), frames)
    first, second, rates, gains = call(
        rims_kernel,
        "rims",
        1.0,
        (message, message, f32(own, LANES), f32(1, frames)),
        (spikes, decay.reshape(own, LANES), frame_gain.reshape(1, frames)),
        [pltpu.SemaphoreType.DMA((4,))],
        far=(0, 1, 2),
        limit=52,
    )
    first, second = swapped(first, second)
    *owns, rows, pay, columns, footprints = call(
        prep_own_kernel,
        "prep_own",
        1.6,
        (split[0],) * 4
        + (f32(3, lines, LANES), f32(2, lines, LANES), f32(2, frames, LANES))
        + (bf16(*footprints.shape),),
        (spikes, rates, gains, footprints),
        [pltpu.VMEM((neurons, frames), F32), pltpu.SemaphoreType.DMA((PARTS + 1,))],
        far=(0, 3),
        limit=44,
    )
    *rims, rows, pay = call(
        prep_rim_kernel,
        "prep_rim",
        0.3,
        (split[1],) * 4 + (f32(3, lines, LANES), f32(2, lines, LANES)),
        (first, second, columns, rows, pay),
    )
    s3, p3, pinv3, z3 = zip(owns, rims)
    constants = lax.all_gather(pay, "tm")
    pays = constants[:, 0]
    scratch = [
        pltpu.VMEM((stripe * K * NEU_BLOCK, frames), F32),
        pltpu.SMEM((stripe, 2 * HB + 1), jnp.int32),
    ]
    zone = (2 * RIM, frames, LANES)
    border = (4 * RIM, frames, LANES)
    for iteration in range(ITERS):
        ends = iteration == ITERS - 1
        ext, zones, spill, send_a, send_b, state = call(
            edge_kernel,
            "edge",
            2.5,
            (
                bf16(chunks * LANES, frames),
                f32(*border),
                f32(*border),
                bf16(*zone),
                bf16(*zone),
                f32(lines, LANES),
            ),
            (pattern, z3, p3, rows, constants, pays, footprints, recording),
            scratch,
            keep=(s3[0],) if ends else (),
        )
        got_a, got_b = swapped(send_a, send_b)
        held = (s3[0], z3[0], state) if ends else ()
        r_inner, pay = call(
            inner_kernel,
            "inner",
            4.0,
            (f32(chunks - 4 * RIM, frames, LANES), f32(2, lines, LANES)),
            (pattern, p3, pinv3, rows, ext, spill, footprints, recording),
            scratch,
            keep=held,
        )
        r_border, pay = call(
            border_kernel,
            "border",
            0.3,
            (f32(*border), f32(2, lines, LANES)),
            (zones, got_a, got_b, p3, pinv3, rows, pay),
            keep=held,
        )
        pays = lax.all_gather(pay, "tm")
        g3, stats = call(
            direction_kernel,
            "direction",
            4.0,
            (f32(chunks, frames, LANES), f32(devices, 2, LANES)),
            (pattern, r_inner, r_border, p3, pinv3, rows, constants, pays, footprints),
            [pltpu.VMEM((chunks * LANES, frames), BF16)],
            keep=held,
        )
        stats = lax.all_to_all(stats, ("tile", "tm"), 0, 0)
        if ends:
            traces = call(
                traces_kernel,
                "traces",
                1.4,
                f32(neurons, frames),
                (z3[0], p3[0], state),
                keep=(s3[0], g3),
            )
            out = call(
                final_kernel,
                "final",
                1.4,
                f32(neurons, frames),
                (s3[0], g3, stats),
                [pltpu.VMEM((neurons, frames), F32), pltpu.SemaphoreType.DMA((PARTS,))],
                far_out=True,
            )
            return out, traces
        s3, z3, pay = call(
            update_kernel,
            "update",
            0.6,
            (split if iteration < ITERS - 2 else split[:1], split, f32(lines, LANES)),
            (s3, g3, stats, p3, pinv3, rows),
        )
        pays = lax.all_gather(pay, "tm")


def solution(mesh):
    return jax.shard_map(
        per_device,
        mesh=mesh,
        in_specs=(
            P("tile", "tm"),
            P("tile", None),
            P("tile", None),
            P("tile"),
            P("tm"),
            P("tile", "tm"),
        ),
        out_specs=(P("tile", "tm"), P("tile", "tm")),
        check_vma=False,
    )
```

profile of v0, /device:TPU:0, one launch (start us, length us, event | category | flops | bytes accessed | tf_op | source)
XLA Modules:
  0.0 87.0 jit_solution(11883529246044023723)
XLA Ops:
  0.6 0.0 copy-start.4
  0.6 1.2 %copy-done.4 = f32[2048,128]{1,0:T(8,128)S(1)} copy-done((f32[2048,128]{1,0:T(8,128)S(1)}, f32[2048,128]{1,0:T(8,128)}, u32[]{:S(2)}) %copy-start.4) | copy-done | bytes 1048600
  1.9 0.0 copy-start.7
  1.9 0.7 copy-done.7
  2.6 0.0 copy-start.8
  2.6 0.7 copy-done.8
  3.2 0.2 rims.1
  3.4 3.0 %collective-permute-start = (f32[136,128]{1,0:T(8,128)S(1)}, f32[136,128]{1,0:T(8,128)S(1)}, u32[]{:S(2)}, u32[]{:S(2)}) collective-permute-start(f32[136,128]{1,0:T(8,128)S(1)} %get-tuple-element.50), channel_id=1, source_target_pairs={{0,1},{2,3},{4,5},{6,7},{1,0},{3,2},{5,4},{7,6},{8,9},{10,11},{12,... | collective-permute-start | bytes 208904 | tf_op jit(solution)/shard_map/ppermute | solution.py:469
  6.5 0.7 collective-permute-start.1
  7.1 0.0 copy-start.5
  7.1 1.2 %copy-done.5 = f32[2048,128]{1,0:T(8,128)S(1)} copy-done((f32[2048,128]{1,0:T(8,128)S(1)}, f32[2048,128]{1,0:T(8,128)}, u32[]{:S(2)}) %copy-start.5) | copy-done | bytes 1048600
  8.3 0.0 copy-start
  8.3 0.0 copy-start.6
  8.3 2.4 %prep_own.1 = (f32[16,128,128]{2,1,0:T(8,128)S(1)}, f32[16,128,128]{2,1,0:T(8,128)S(1)}, f32[16,128,128]{2,1,0:T(8,128)S(1)}, f32[16,128,128]{2,1,0:T(8,128)S(1)...) custom-call(f32[2048,128]{1,0:T(8,128)S(1)} %copy-done.5, ...), custom_call_target="tpu_custom_call" | custom-call | flops 160000000 | bytes 4800000 | tf_op jit(solution)/shard_map/prep_own/pallas_call | solution.py:448
  10.8 0.0 collective-permute-done.refs_0_
  10.8 0.0 collective-permute-done.1.refs_1_
  10.8 0.3 prep_rim.1
  11.1 5.3 %all-gather = f32[8,24,128]{2,1,0:T(8,128)S(1)} all-gather(f32[2,24,128]{2,1,0:T(8,128)S(1)} %get-tuple-element.63), channel_id=2, replica_groups=mesh['tm'=4,'tile'=8] {'tm'}, dimensions={0}, use_global_device_ids=true | all-gather | bytes 122880 | tf_op jit(solution)/shard_map/all_gather | solution.py:513
  16.4 0.0 copy-done
  16.4 0.0 copy-done.6
  16.4 2.5 %edge.2 = (bf16[2304,128]{1,0:T(8,128)(2,1)S(1)}, f32[4,128,128]{2,1,0:T(8,128)S(1)}, f32[4,128,128]{2,1,0:T(8,128)S(1)}, bf16[2,128,128]{2,1,0:T(8,128)(2,1)S(1...) custom-call(s32[4,32]{1,0:T(4,128)S(1)} %bitcast.17, f32[16,128,128]{2,1,0:T(8,128)S(1)} %get-tuple-element.61.refs_1__0_, ...), custom_call_target="tpu_custom_call" | custom-call | flops 250000000 | bytes 7500000 | tf_op jit(solution)/shard_map/edge/pallas_call | solution.py:448
  18.9 4.3 %collective-permute-start.2 = (bf16[2,128,128]{2,1,0:T(8,128)(2,1)S(1)}, bf16[2,128,128]{2,1,0:T(8,128)(2,1)S(1)}, u32[]{:S(2)}, u32[]{:S(2)}) collective-permute-start(bf16[2,128,128]{2,1,0:T(8,128)(2,1)S(1)} %get-tuple-element.69), channel_id=1, source_target_pairs={{0,1},{2,3},{4,5},{6,7},{1,0},{3,2},{5,4},{7,6},{8,9},{10,11},{12,... | collective-permute-start | bytes 196616 | tf_op jit(solution)/shard_map/ppermute | solution.py:469
  23.2 0.7 collective-permute-start.3
  23.9 3.3 %inner.2 = (f32[14,128,128]{2,1,0:T(8,128)S(1)}, f32[2,24,128]{2,1,0:T(8,128)S(1)}) custom-call(s32[4,32]{1,0:T(4,128)S(1)} %bitcast.18, f32[16,128,128]{2,1,0:T(8,128)S(1)} %get-tuple-element.56.refs_2__0_.refs_1__0_.refs_3__0_.refs_1_, f32[2,128,128]{2,1,0:T(8,128)S(1)} %get-tuple-element.57.refs_2__1_.refs_1__1_.refs_3__1_, ...), custom_call_target="tpu_custom_call" | custom-call | flops 400000000 | bytes 12000000 | tf_op jit(solution)/shard_map/inner/pallas_call | solution.py:448
  27.2 0.0 collective-permute-done.2.refs_1_
  27.2 0.0 collective-permute-done.3.refs_2_
  27.2 0.3 border.2
  27.5 5.3 %all-gather.1 = f32[8,24,128]{2,1,0:T(8,128)S(1)} all-gather(f32[2,24,128]{2,1,0:T(8,128)S(1)} %get-tuple-element.73), channel_id=3, replica_groups=mesh['tm'=4,'tile'=8] {'tm'}, dimensions={0}, use_global_device_ids=true | all-gather | bytes 122880 | tf_op jit(solution)/shard_map/all_gather | solution.py:558
  32.8 2.8 %direction.2 = (f32[18,128,128]{2,1,0:T(8,128)S(1)}, f32[32,2,128]{2,1,0:T(2,128)S(1)}) custom-call(s32[4,32]{1,0:T(4,128)S(1)} %bitcast.19, f32[14,128,128]{2,1,0:T(8,128)S(1)} %get-tuple-element.67.refs_1_, f32[4,128,128]{2,1,0:T(8,128)S(1)} %get-tuple-element.72.refs_2_, f32[16,128,128]{2,1,0:T(8,128)S(1)} %get-tuple-element.56.refs_2__0_.refs_1__0_.refs_3__0_.refs_1_, ...), custom_call_target="tpu_custom_call" | custom-call | flops 400000000 | bytes 12000000 | tf_op jit(solution)/shard_map/direction/pallas_call | solution.py:448
  35.6 14.0 %all_to_all.10.refs_2_ = f32[32,2,128]{2,1,0:T(2,128)S(1)} all-to-all(f32[32,2,128]{2,1,0:T(2,128)S(1)} %get-tuple-element.75), channel_id=1, replica_groups=mesh['tm'=4,'tile'=8] {'tile','tm'}, dimensions={0} | all-to-all | bytes 65536 | tf_op jit(solution)/shard_map/all_to_all | solution.py:568
  49.6 0.7 update.1
  50.3 5.2 %all-gather.2 = f32[96,128]{1,0:T(8,128)S(1)} all-gather(f32[24,128]{1,0:T(8,128)S(1)} %get-tuple-element.79), channel_id=4, replica_groups=mesh['tm'=4,'tile'=8] {'tm'}, dimensions={0}, use_global_device_ids=true | all-gather | bytes 61440 | tf_op jit(solution)/shard_map/all_gather | solution.py:595
  55.5 1.9 %edge.3 = (bf16[2304,128]{1,0:T(8,128)(2,1)S(1)}, f32[4,128,128]{2,1,0:T(8,128)S(1)}, f32[4,128,128]{2,1,0:T(8,128)S(1)}, bf16[2,128,128]{2,1,0:T(8,128)(2,1)S(1...) custom-call(s32[4,32]{1,0:T(4,128)S(1)} %bitcast.20, ...), custom_call_target="tpu_custom_call" | custom-call | flops 250000000 | bytes 7500000 | tf_op jit(solution)/shard_map/edge/pallas_call | solution.py:448
  57.5 0.6 collective-permute-start.4
  58.1 0.8 collective-permute-start.5
  58.9 3.3 %inner.3 = (f32[14,128,128]{2,1,0:T(8,128)S(1)}, f32[2,24,128]{2,1,0:T(8,128)S(1)}) custom-call(s32[4,32]{1,0:T(4,128)S(1)} %bitcast.21, f32[16,128,128]{2,1,0:T(8,128)S(1)} %get-tuple-element.56.refs_2__0_.refs_1__0_.refs_3__0_.refs_1_, f32[2,128,128]{2,1,0:T(8,128)S(1)} %get-tuple-element.57.refs_2__1_.refs_1__1_.refs_3__1_, ...), custom_call_target="tpu_custom_call" | custom-call | flops 400000000 | bytes 12000000 | tf_op jit(solution)/shard_map/inner/pallas_call | solution.py:448
  62.2 0.0 collective-permute-done.4.refs_1_
  62.2 0.0 collective-permute-done.5.refs_2_
  62.2 0.3 border.3
  62.5 5.3 %all-gather.3 = f32[8,24,128]{2,1,0:T(8,128)S(1)} all-gather(f32[2,24,128]{2,1,0:T(8,128)S(1)} %get-tuple-element.89), channel_id=5, replica_groups=mesh['tm'=4,'tile'=8] {'tm'}, dimensions={0}, use_global_device_ids=true | all-gather | bytes 122880 | tf_op jit(solution)/shard_map/all_gather | solution.py:558
  67.8 3.4 %direction.3 = (f32[18,128,128]{2,1,0:T(8,128)S(1)}, f32[32,2,128]{2,1,0:T(2,128)}) custom-call(s32[4,32]{1,0:T(4,128)S(1)} %bitcast.22, f32[14,128,128]{2,1,0:T(8,128)S(1)} %get-tuple-element.83.refs_1_, f32[4,128,128]{2,1,0:T(8,128)S(1)} %get-tuple-element.88.refs_2_, f32[16,128,128]{2,1,0:T(8,128)S(1)} %get-tuple-element.56.refs_2__0_.refs_1__0_.refs_3__0_.refs_1_, ...), custom_call_target="tpu_custom_call" | custom-call | flops 400000000 | bytes 12000000 | tf_op jit(solution)/shard_map/direction/pallas_call | solution.py:448
  71.2 0.0 copy-start.1
  71.2 1.0 %copy-done.1 = f32[18,128,128]{2,1,0:T(8,128)} copy-done((f32[18,128,128]{2,1,0:T(8,128)}, f32[18,128,128]{2,1,0:T(8,128)S(1)}, u32[]{:S(2)}) %copy-start.1) | copy-done | bytes 1179672
  72.2 4.8 %all-to-all-start.1 = ((f32[32,2,128]{2,1,0:T(2,128)}), f32[32,2,128]{2,1,0:T(2,128)S(1)}, u32[]{:S(2)}, u32[]{:S(2)}) async-start(f32[32,2,128]{2,1,0:T(2,128)} %get-tuple-element.91), calls=%async_computation.1 | async-start | bytes 65536 | tf_op jit(solution)/shard_map/all_to_all | solution.py:568
  77.0 0.0 copy-start.2
  77.1 1.3 %copy-done.2 = f32[18,128,128]{2,1,0:T(8,128)S(1)} copy-done((f32[18,128,128]{2,1,0:T(8,128)S(1)}, f32[18,128,128]{2,1,0:T(8,128)}, u32[]{:S(2)}) %copy-start.2) | copy-done | bytes 1179672
  78.3 1.3 %traces.1 = f32[2048,128]{1,0:T(8,128)} custom-call(f32[16,128,128]{2,1,0:T(8,128)S(1)} %get-tuple-element.77.refs_1__0_.refs_8__1_.refs_7__1_.refs_9__1_.refs_0_, f32[16,128,128]{2,1,0:T(8,128)S(1)} %get-tuple-element.56.refs_2__0_.refs_1__0_.refs_3__0_.refs_1_, f32[24,128]{1,0:T(8,128)S(1)} %get-tuple-element.82.refs_8__2_.refs_7__2_.refs_9__2_.refs_2_, ...), custom_call_target="tpu_custom_call" | custom-call | flops 140000000 | bytes 4200000 | tf_op jit(solution)/shard_map/traces/pallas_call | solution.py:448
  79.6 4.7 %all-to-all-done.1.refs_2_ = f32[32,2,128]{2,1,0:T(2,128)S(1)} async-done(((f32[32,2,128]{2,1,0:T(2,128)}), f32[32,2,128]{2,1,0:T(2,128)S(1)}, u32[]{:S(2)}, u32[]{:S(2)}) %all-to-all-start.1) | async-done | bytes 32800 | tf_op jit(solution)/shard_map/all_to_all | solution.py:568
  84.3 0.0 copy-start.3
  84.3 1.3 %copy-done.3 = f32[18,128,128]{2,1,0:T(8,128)S(1)} copy-done((f32[18,128,128]{2,1,0:T(8,128)S(1)}, f32[18,128,128]{2,1,0:T(8,128)}, u32[]{:S(2)}) %copy-start.3) | copy-done | bytes 1179672
  85.6 1.3 %final.1 = f32[2048,128]{1,0:T(8,128)} custom-call(f32[16,128,128]{2,1,0:T(8,128)S(1)} %get-tuple-element.76.refs_8__0_.refs_7__0_.refs_9__0_.refs_0_.refs_3__0_, f32[18,128,128]{2,1,0:T(8,128)S(1)} %copy-done.3, f32[32,2,128]{2,1,0:T(2,128)S(1)} %all-to-all-done.1.refs_2_), custom_call_target="tpu_custom_call" | custom-call | flops 140000000 | bytes 4200000 | tf_op jit(solution)/shard_map/final/pallas_call | solution.py:448
  (1 shorter events, 0.0 us)
Async XLA Ops:
  0.6 1.2 %copy-start.4 = (f32[2048,128]{1,0:T(8,128)S(1)}, f32[2048,128]{1,0:T(8,128)}, u32[]{:S(2)}) copy-start(f32[2048,128]{1,0:T(8,128)} %refs_0_.3) | copy-start | bytes 3145732
  1.9 0.7 copy-start.7
  2.6 0.7 copy-start.8
  3.4 7.4 %collective-permute-start = (f32[136,128]{1,0:T(8,128)S(1)}, f32[136,128]{1,0:T(8,128)S(1)}, u32[]{:S(2)}, u32[]{:S(2)}) collective-permute-start(f32[136,128]{1,0:T(8,128)S(1)} %get-tuple-element.50), channel_id=1, source_target_pairs={{0,1},{2,3},{4,5},{6,7},{1,0},{3,2},{5,4},{7,6},{8,9},{10,11},{12,... | collective-permute-start | bytes 208904 | tf_op jit(solution)/shard_map/ppermute | solution.py:469
  6.5 4.4 %collective-permute-start.1 = (f32[136,128]{1,0:T(8,128)S(1)}, f32[136,128]{1,0:T(8,128)S(1)}, u32[]{:S(2)}, u32[]{:S(2)}) collective-permute-start(f32[136,128]{1,0:T(8,128)S(1)} %get-tuple-element.51), channel_id=1, source_target_pairs={{1,2},{3,4},{5,6},{2,1},{4,3},{6,5},{9,10},{11,12},{13,14},{10,9},... | collective-permute-start | bytes 208904 | tf_op jit(solution)/shard_map/ppermute | solution.py:469
  7.1 1.2 %copy-start.5 = (f32[2048,128]{1,0:T(8,128)S(1)}, f32[2048,128]{1,0:T(8,128)}, u32[]{:S(2)}) copy-start(f32[2048,128]{1,0:T(8,128)} %refs_0_.3) | copy-start | bytes 3145732
  8.3 8.1 %copy-start = (bf16[8192,128]{1,0:T(8,128)(2,1)S(1)}, bf16[8192,128]{1,0:T(8,128)(2,1)}, u32[]{:S(2)}) copy-start(bf16[8192,128]{1,0:T(8,128)(2,1)} %refs_7_.7) | copy-start | bytes 6291460
  8.3 8.1 %copy-start.6 = (s32[32,4]{0,1:T(4,128)S(1)}, s32[32,4]{0,1:T(4,128)}, u32[]{:S(2)}) copy-start(s32[32,4]{0,1:T(4,128)} %param.8) | copy-start | bytes 1540
  18.9 8.2 %collective-permute-start.2 = (bf16[2,128,128]{2,1,0:T(8,128)(2,1)S(1)}, bf16[2,128,128]{2,1,0:T(8,128)(2,1)S(1)}, u32[]{:S(2)}, u32[]{:S(2)}) collective-permute-start(bf16[2,128,128]{2,1,0:T(8,128)(2,1)S(1)} %get-tuple-element.69), channel_id=1, source_target_pairs={{0,1},{2,3},{4,5},{6,7},{1,0},{3,2},{5,4},{7,6},{8,9},{10,11},{12,... | collective-permute-start | bytes 196616 | tf_op jit(solution)/shard_map/ppermute | solution.py:469
  23.2 4.0 %collective-permute-start.3 = (bf16[2,128,128]{2,1,0:T(8,128)(2,1)S(1)}, bf16[2,128,128]{2,1,0:T(8,128)(2,1)S(1)}, u32[]{:S(2)}, u32[]{:S(2)}) collective-permute-start(bf16[2,128,128]{2,1,0:T(8,128)(2,1)S(1)} %get-tuple-element.70), channel_id=1, source_target_pairs={{1,2},{3,4},{5,6},{2,1},{4,3},{6,5},{9,10},{11,12},{13,14},{10,9},... | collective-permute-start | bytes 196616 | tf_op jit(solution)/shard_map/ppermute | solution.py:469
  57.5 4.7 %collective-permute-start.4 = (bf16[2,128,128]{2,1,0:T(8,128)(2,1)S(1)}, bf16[2,128,128]{2,1,0:T(8,128)(2,1)S(1)}, u32[]{:S(2)}, u32[]{:S(2)}) collective-permute-start(bf16[2,128,128]{2,1,0:T(8,128)(2,1)S(1)} %get-tuple-element.85), channel_id=1, source_target_pairs={{0,1},{2,3},{4,5},{6,7},{1,0},{3,2},{5,4},{7,6},{8,9},{10,11},{12,... | collective-permute-start | bytes 196616 | tf_op jit(solution)/shard_map/ppermute | solution.py:469
  58.1 4.1 %collective-permute-start.5 = (bf16[2,128,128]{2,1,0:T(8,128)(2,1)S(1)}, bf16[2,128,128]{2,1,0:T(8,128)(2,1)S(1)}, u32[]{:S(2)}, u32[]{:S(2)}) collective-permute-start(bf16[2,128,128]{2,1,0:T(8,128)(2,1)S(1)} %get-tuple-element.86), channel_id=1, source_target_pairs={{1,2},{3,4},{5,6},{2,1},{4,3},{6,5},{9,10},{11,12},{13,14},{10,9},... | collective-permute-start | bytes 196616 | tf_op jit(solution)/shard_map/ppermute | solution.py:469
  71.2 1.0 %copy-start.1 = (f32[18,128,128]{2,1,0:T(8,128)}, f32[18,128,128]{2,1,0:T(8,128)S(1)}, u32[]{:S(2)}) copy-start(f32[18,128,128]{2,1,0:T(8,128)S(1)} %get-tuple-element.90.refs_1_.refs_3__1_) | copy-start | bytes 3538948
  72.2 12.1 %all-to-all-start.1 = ((f32[32,2,128]{2,1,0:T(2,128)}), f32[32,2,128]{2,1,0:T(2,128)S(1)}, u32[]{:S(2)}, u32[]{:S(2)}) async-start(f32[32,2,128]{2,1,0:T(2,128)} %get-tuple-element.91), calls=%async_computation.1 | async-start | bytes 65536 | tf_op jit(solution)/shard_map/all_to_all | solution.py:568
  77.0 1.3 %copy-start.2 = (f32[18,128,128]{2,1,0:T(8,128)S(1)}, f32[18,128,128]{2,1,0:T(8,128)}, u32[]{:S(2)}) copy-start(f32[18,128,128]{2,1,0:T(8,128)} %copy-done.1) | copy-start | bytes 3538948
  84.3 1.3 %copy-start.3 = (f32[18,128,128]{2,1,0:T(8,128)S(1)}, f32[18,128,128]{2,1,0:T(8,128)}, u32[]{:S(2)}) copy-start(f32[18,128,128]{2,1,0:T(8,128)} %copy-done.1) | copy-start | bytes 3538948
where the time goes:
time: 87.5 us; the launch traced here: 87 us
  blocking collectives  35.3 us (40%)
  Pallas kernels  23.8 us (27%)
  starting transfers between devices  14.9 us (17%)
  local copies, waits for them, and re-layouts  7.38 us (8%)
  waiting for transfers between devices  4.68 us (5%)
  between operations  0.97 us (1%)
    pallas_call x14, Pallas kernels, call(): pl.pallas_call(body, name=name, out_shape=outs, in_specs=in_specs, out_sp...  23.8 us
    all_gather x3, blocking collectives, per_device(): pays = lax.all_gather(pay, 'tm')  15.9 us
    all_to_all x1, blocking collectives, per_device(): stats = lax.all_to_all(stats, ('tile', 'tm'), 0, 0)  14 us
    ppermute x3, starting transfers between devices, swapped(): lax.ppermute(first, 'tile', pairs(0))  7.94 us
    unnamed x18, local copies, waits for them, and re-layouts  7.38 us
    all_gather x1, blocking collectives, per_device(): constants = lax.all_gather(pay, 'tm')  5.34 us
    all_to_all x1, starting transfers between devices, per_device(): stats = lax.all_to_all(stats, ('tile', 'tm'), 0, 0)  4.79 us
    all_to_all x1, waiting for transfers between devices, per_device(): stats = lax.all_to_all(stats, ('tile', 'tm'), 0, 0)  4.67 us
  transfers between devices with their start and end apart: 7, of which 1 were waited for; matrix products, arithmetic and copies ran while one was open for 0% of the time, Pallas kernels for 12%

commit v1 on v0

--- a/solution.py
+++ b/solution.py
@@ -105,7 +105,7 @@
     return middle, whole, prefix_col, inverse_col
 
 
-def rims_kernel(spikes, decay, gains, first, second, rates_here, gains_here, sems):
+def rims_kernel(spikes, decay, first, second, rates_here, spikes_here, sems):
     edge = RIM * LANES
     neurons = spikes.shape[0]
     own = decay.shape[0]
@@ -114,15 +114,15 @@
     bottom = jnp.where(even, 0, neurons - edge)
     copies = [
         pltpu.make_async_copy(decay, rates_here, sems.at[0]),
-        pltpu.make_async_copy(gains, gains_here, sems.at[1]),
         pltpu.make_async_copy(
-            spikes.at[pl.ds(pl.multiple_of(top, LANES), edge)], first.at[pl.ds(0, edge)], sems.at[2]
+            spikes.at[pl.ds(pl.multiple_of(top, LANES), edge)], first.at[pl.ds(0, edge)], sems.at[1]
         ),
         pltpu.make_async_copy(
             spikes.at[pl.ds(pl.multiple_of(bottom, LANES), edge)],
             second.at[pl.ds(0, edge)],
-            sems.at[3],
+            sems.at[2],
         ),
+        pltpu.make_async_copy(spikes, spikes_here, sems.at[3]),
     ]
     for copy in copies:
         copy.start()
@@ -137,20 +137,11 @@
 
 
 def prep_own_kernel(
-    spikes, decay, gains, feet, s3, p3, pinv3, z3, rows, pay, columns, feet_here, spikes_here, sems
+    spikes, decay, gains, feet, s3, p3, pinv3, z3, rows, pay, columns, feet_here, sem
 ):
     own = s3.shape[0]
     chunks = own + 2 * RIM
-    size = spikes.shape[0] // PARTS
-    copies = [
-        pltpu.make_async_copy(
-            spikes.at[pl.ds(i * size, size)], spikes_here.at[pl.ds(i * size, size)], sems.at[i]
-        )
-        for i in range(PARTS)
-    ]
-    for copy in copies:
-        copy.start()
-    fetch = pltpu.make_async_copy(feet, feet_here, sems.at[PARTS])
+    fetch = pltpu.make_async_copy(feet, feet_here, sem)
     fetch.start()
     middle, whole, prefix_col, inverse_col = gain_columns(gains[...])
     columns[0] = prefix_col
@@ -161,9 +152,7 @@
     pay[0, chunks : chunks + 1, :] = whole
     shared = middle, prefix_col, inverse_col, table(spikes.shape[1], False)
     for i in range(own):
-        if i % (own // PARTS) == 0:
-            copies[i // (own // PARTS)].wait()
-        field = spikes_here[i * LANES : (i + 1) * LANES, :]
+        field = spikes[i * LANES : (i + 1) * LANES, :]
         at = [ref.at[i] for ref in (s3, p3, pinv3, z3)]
         prep_chunk(i + RIM, decay[i : i + 1, :], field, shared, *at, rows, pay)
     fetch.wait()
@@ -286,9 +275,14 @@
 
 
 def edge_kernel(
-    pattern, z3, p3, rows, pay, pays, feet, record, ext, zones, spill, send_a, send_b, state, *scratch
+    pattern, z3, p3, rows, pay, pays, feet, record, ext, zones, spill, send_a, send_b, *rest
 ):
-    contrib, place = scratch
+    if len(rest) > 2:
+        traces, contrib, place, traces_here, sems = rest
+    else:
+        contrib, place = rest
+        traces = None
+    copies = []
     chunks = chunk_count(z3)
     stripe = pattern.shape[1]
     edge = 2 * HB
@@ -298,10 +292,19 @@
     for m in range(pays.shape[0]):
         carry = jnp.where(m < me, pays[m] + totals[m] * carry, carry)
     carry = carry * rows[1]
-    state[...] = carry
     for c in range(chunks):
-        field = chunk(p3, c)[...] * (chunk(z3, c)[...] + carry[c : c + 1, :])
-        ext[c * LANES : (c + 1) * LANES, :] = field.T.astype(BF16)
+        field = (chunk(p3, c)[...] * (chunk(z3, c)[...] + carry[c : c + 1, :])).T
+        ext[c * LANES : (c + 1) * LANES, :] = field.astype(BF16)
+        if traces is not None and RIM <= c < chunks - RIM:
+            part = (chunks - 2 * RIM) // PARTS
+            i = c - RIM
+            traces_here[i * LANES : (i + 1) * LANES, :] = field
+            if (i + 1) % part == 0:
+                at = pl.ds((i + 1 - part) * LANES, part * LANES)
+                copies.append(
+                    pltpu.make_async_copy(traces_here.at[at], traces.at[at], sems.at[i // part])
+                )
+                copies[-1].start()
     ranges = ((0, edge), (stripe - edge, stripe))
     for start, stop in ranges:
         pull_back(pattern, ext, feet, record, contrib, place, start, stop)
@@ -315,6 +318,8 @@
         send_b[i] = jnp.where(even, below, above).astype(BF16)
         spill[i] = gathered(contrib, place, 2 * RIM + i, ranges)
         spill[2 * RIM + i] = gathered(contrib, place, chunks - 4 * RIM + i, ranges)
+    for copy in copies:
+        copy.wait()
 
 
 def adjoint_chunk(sums_table, field, p, pinv, rows, c, r3, pay):
@@ -416,13 +421,6 @@
     stats[...] = jnp.broadcast_to(both[None], stats.shape)
 
 
-def traces_kernel(z3, p3, state, traces):
-    for i in range(z3.shape[0]):
-        c = i + RIM
-        field = p3[i] * (z3[i] + state[c : c + 1, :])
-        traces[i * LANES : (i + 1) * LANES, :] = field.T
-
-
 def f32(*shape):
     return jax.ShapeDtypeStruct(shape, F32)
 
@@ -432,7 +430,7 @@
 
 
 def call(
-    kernel, name, micros, outs, args, scratch=(), far=(), far_out=False, keep=(), limit=16
+    kernel, name, micros, outs, args, scratch=(), far=(), far_out=(), keep=(), limit=16
 ):
     def spec(place, arg):
         if place in far:
@@ -450,7 +448,10 @@
         name=name,
         out_shape=outs,
         in_specs=in_specs,
-        out_specs=jax.tree.map(lambda _: HBM if far_out else VMEM, outs),
+        out_specs=tuple(
+            jax.tree.map(lambda _: HBM if place in far_out else VMEM, out)
+            for place, out in enumerate(outs)
+        ),
         scratch_shapes=scratch,
         compiler_params=pltpu.CompilerParams(vmem_limit_bytes=int(limit * 2**20)),
         cost_estimate=pl.CostEstimate(
@@ -479,14 +480,15 @@
     devices = lax.axis_size("tile") * lax.axis_size("tm")
     split = (f32(own, frames, LANES), f32(2 * RIM, frames, LANES))
     message = f32(RIM * LANES + padded8(RIM), frames)
-    first, second, rates, gains = call(
+    gains = frame_gain.reshape(1, frames)
+    first, second, rates, spikes = call(
         rims_kernel,
         "rims",
         1.0,
-        (message, message, f32(own, LANES), f32(1, frames)),
-        (spikes, decay.reshape(own, LANES), frame_gain.reshape(1, frames)),
+        (message, message, f32(own, LANES), f32(neurons, frames)),
+        (spikes, decay.reshape(own, LANES)),
         [pltpu.SemaphoreType.DMA((4,))],
-        far=(0, 1, 2),
+        far=(0, 1),
         limit=52,
     )
     first, second = swapped(first, second)
@@ -498,8 +500,8 @@
         + (f32(3, lines, LANES), f32(2, lines, LANES), f32(2, frames, LANES))
         + (bf16(*footprints.shape),),
         (spikes, rates, gains, footprints),
-        [pltpu.VMEM((neurons, frames), F32), pltpu.SemaphoreType.DMA((PARTS + 1,))],
-        far=(0, 3),
+        [pltpu.SemaphoreType.DMA],
+        far=(3,),
         limit=44,
     )
     *rims, rows, pay = call(
@@ -516,11 +518,12 @@
         pltpu.VMEM((stripe * K * NEU_BLOCK, frames), F32),
         pltpu.SMEM((stripe, 2 * HB + 1), jnp.int32),
     ]
+    staged = [pltpu.VMEM((neurons, frames), F32), pltpu.SemaphoreType.DMA((PARTS,))]
     zone = (2 * RIM, frames, LANES)
     border = (4 * RIM, frames, LANES)
     for iteration in range(ITERS):
         ends = iteration == ITERS - 1
-        ext, zones, spill, send_a, send_b, state = call(
+        ext, zones, spill, send_a, send_b, *traces = call(
             edge_kernel,
             "edge",
             2.5,
@@ -530,14 +533,15 @@
                 f32(*border),
                 bf16(*zone),
                 bf16(*zone),
-                f32(lines, LANES),
-            ),
+            )
+            + ((f32(neurons, frames),) if ends else ()),
             (pattern, z3, p3, rows, constants, pays, footprints, recording),
-            scratch,
+            scratch + (staged if ends else []),
+            far_out=(5,),
             keep=(s3[0],) if ends else (),
         )
         got_a, got_b = swapped(send_a, send_b)
-        held = (s3[0], z3[0], state) if ends else ()
+        held = (s3[0],) if ends else ()
         r_inner, pay = call(
             inner_kernel,
             "inner",
@@ -567,24 +571,16 @@
         )
         stats = lax.all_to_all(stats, ("tile", "tm"), 0, 0)
         if ends:
-            traces = call(
-                traces_kernel,
-                "traces",
-                1.4,
-                f32(neurons, frames),
-                (z3[0], p3[0], state),
-                keep=(s3[0], g3),
-            )
-            out = call(
+            (out,) = call(
                 final_kernel,
                 "final",
                 1.4,
-                f32(neurons, frames),
+                (f32(neurons, frames),),
                 (s3[0], g3, stats),
-                [pltpu.VMEM((neurons, frames), F32), pltpu.SemaphoreType.DMA((PARTS,))],
-                far_out=True,
+                staged,
+                far_out=(0,),
             )
-            return out, traces
+            return out, traces[0]
         s3, z3, pay = call(
             update_kernel,
             "update",

time: 87.5 us -> 84.3 us (0.963)
  blocking collectives: 35.3 us -> 47.1 us
  local copies, waits for them, and re-layouts: 7.38 us -> 1.35 us
  starting transfers between devices: 14.9 us -> 10.1 us
  waiting for transfers between devices: 4.68 us -> 0.02 us
    all_to_all x1 -> x2, blocking collectives: 14 us -> 25.8 us  [per_device(): stats = lax.all_to_all(stats, ('tile', 'tm'), 0, 0)]
    unnamed x18 -> x8, local copies, waits for them, and re-layouts: 7.38 us -> 1.35 us
    all_to_all x1 -> x0, starting transfers between devices: 4.79 us -> none  [per_device(): stats = lax.all_to_all(stats, ('tile', 'tm'), 0, 0)]
    all_to_all x1 -> x0, waiting for transfers between devices: 4.67 us -> none  [per_device(): stats = lax.all_to_all(stats, ('tile', 'tm'), 0, 0)]
    pallas_call x14 -> x13, Pallas kernels: 23.8 us -> 24.4 us  [call(): pl.pallas_call(body, name=name, out_shape=outs, in_specs=in_specs, out_sp...]
  transfers between devices with their start and end apart: 7 -> 6, of which waited for: 1 -> 0; matrix products, arithmetic and copies ran while one was open for 0% -> 0% of each run, Pallas kernels for 12% -> 12%
where the time goes in v1:
time: 84.3 us; the launch traced here: 84 us
  blocking collectives  47.1 us (56%)
  Pallas kernels  24.4 us (29%)
  starting transfers between devices  10.1 us (12%)
  local copies, waits for them, and re-layouts  1.35 us (2%)
  between operations  0.97 us (1%)
    all_to_all x2, blocking collectives, per_device(): stats = lax.all_to_all(stats, ('tile', 'tm'), 0, 0)  25.8 us
    pallas_call x13, Pallas kernels, call(): pl.pallas_call(body, name=name, out_shape=outs, in_specs=in_specs, out_sp...  24.4 us
    all_gather x3, blocking collectives, per_device(): pays = lax.all_gather(pay, 'tm')  15.9 us
    ppermute x3, starting transfers between devices, swapped(): lax.ppermute(first, 'tile', pairs(0))  8.01 us
    all_gather x1, blocking collectives, per_device(): constants = lax.all_gather(pay, 'tm')  5.34 us
    ppermute x3, starting transfers between devices, swapped(): lax.ppermute(second, 'tile', pairs(1))  2.14 us
  transfers between devices with their start and end apart: 6, of which 0 were waited for; matrix products, arithmetic and copies ran while one was open for 0% of the time, Pallas kernels for 12%

profile of v1, /device:TPU:0, one launch (start us, length us, event | category | flops | bytes accessed | tf_op | source)
XLA Modules:
  0.0 84.0 jit_solution(1823923761574064249)
XLA Ops:
  0.6 0.0 copy-start.2
  0.6 0.7 copy-done.2
  1.3 1.4 %rims.1 = (f32[136,128]{1,0:T(8,128)S(1)}, f32[136,128]{1,0:T(8,128)S(1)}, f32[16,128]{1,0:T(8,128)S(1)}, f32[2048,128]{1,0:T(8,128)S(1)}) custom-call(f32[2048,128]{1,0:T(8,128)} %refs_0_.1, f32[16,128]{1,0:T(8,128)S(1)} %bitcast.23), custom_call_target="tpu_custom_call" | custom-call | flops 100000000 | bytes 3000000 | tf_op jit(solution)/shard_map/rims/pallas_call | solution.py:446
  2.7 3.0 %collective-permute-start = (f32[136,128]{1,0:T(8,128)S(1)}, f32[136,128]{1,0:T(8,128)S(1)}, u32[]{:S(2)}, u32[]{:S(2)}) collective-permute-start(f32[136,128]{1,0:T(8,128)S(1)} %get-tuple-element.50), channel_id=1, source_target_pairs={{0,1},{2,3},{4,5},{6,7},{1,0},{3,2},{5,4},{7,6},{8,9},{10,11},{12,... | collective-permute-start | bytes 208904 | tf_op jit(solution)/shard_map/ppermute | solution.py:470
  5.7 0.7 collective-permute-start.1
  6.4 0.0 copy-start.3
  6.4 0.6 copy-done.3
  7.0 0.0 copy-start
  7.0 0.0 copy-start.1
  7.0 3.4 %prep_own.1 = (f32[16,128,128]{2,1,0:T(8,128)S(1)}, f32[16,128,128]{2,1,0:T(8,128)S(1)}, f32[16,128,128]{2,1,0:T(8,128)S(1)}, f32[16,128,128]{2,1,0:T(8,128)S(1)...) custom-call(f32[2048,128]{1,0:T(8,128)S(1)} %get-tuple-element.47.re, ...), custom_call_target="tpu_custom_call" | custom-call | flops 160000000 | bytes 4800000 | tf_op jit(solution)/shard_map/prep_own/pallas_call | solution.py:446
  10.5 0.0 collective-permute-done.refs_0_
  10.5 0.0 collective-permute-done.1.refs_1_
  10.5 0.3 prep_rim.1
  10.8 5.3 %all-gather = f32[8,24,128]{2,1,0:T(8,128)S(1)} all-gather(f32[2,24,128]{2,1,0:T(8,128)S(1)} %get-tuple-element.63), channel_id=2, replica_groups=mesh['tm'=4,'tile'=8] {'tm'}, dimensions={0}, use_global_device_ids=true | all-gather | bytes 122880 | tf_op jit(solution)/shard_map/all_gather | solution.py:515
  16.1 0.0 copy-done
  16.1 0.0 copy-done.1
  16.1 1.9 %edge.2 = (bf16[2304,128]{1,0:T(8,128)(2,1)S(1)}, f32[4,128,128]{2,1,0:T(8,128)S(1)}, f32[4,128,128]{2,1,0:T(8,128)S(1)}, bf16[2,128,128]{2,1,0:T(8,128)(2,1)S(1)}, bf16[2,128,128]{2,1,0:T(8,128)(2,1)S(1)}) custom-call(s32[4,32]{1,0:T(4,128)S(1)} %bitcast.17, f32[16,128,128]{2,1,0:T(8,128)S(1)} %get-tuple-element.61.refs_1__0_, ...), custom_call_target="tpu_custom_call" | custom-call | flops 250000000 | bytes 7500000 | tf_op jit(solution)/shard_map/edge/pallas_call | solution.py:446
  18.1 4.3 %collective-permute-start.2 = (bf16[2,128,128]{2,1,0:T(8,128)(2,1)S(1)}, bf16[2,128,128]{2,1,0:T(8,128)(2,1)S(1)}, u32[]{:S(2)}, u32[]{:S(2)}) collective-permute-start(bf16[2,128,128]{2,1,0:T(8,128)(2,1)S(1)} %get-tuple-element.69), channel_id=1, source_target_pairs={{0,1},{2,3},{4,5},{6,7},{1,0},{3,2},{5,4},{7,6},{8,9},{10,11},{12,... | collective-permute-start | bytes 196616 | tf_op jit(solution)/shard_map/ppermute | solution.py:470
  22.4 0.7 collective-permute-start.3
  23.1 3.3 %inner.2 = (f32[14,128,128]{2,1,0:T(8,128)S(1)}, f32[2,24,128]{2,1,0:T(8,128)S(1)}) custom-call(s32[4,32]{1,0:T(4,128)S(1)} %bitcast.18, f32[16,128,128]{2,1,0:T(8,128)S(1)} %get-tuple-element.56.refs_2__0_.refs_1__0_.refs_3__0_, f32[2,128,128]{2,1,0:T(8,128)S(1)} %get-tuple-element.57.refs_2__1_.refs_1__1_.refs_3__1_, ...), custom_call_target="tpu_custom_call" | custom-call | flops 400000000 | bytes 12000000 | tf_op jit(solution)/shard_map/inner/pallas_call | solution.py:446
  26.4 0.0 collective-permute-done.2.refs_1_
  26.4 0.0 collective-permute-done.3.refs_2_
  26.4 0.3 border.2
  26.7 5.3 %all-gather.1 = f32[8,24,128]{2,1,0:T(8,128)S(1)} all-gather(f32[2,24,128]{2,1,0:T(8,128)S(1)} %get-tuple-element.73), channel_id=3, replica_groups=mesh['tm'=4,'tile'=8] {'tm'}, dimensions={0}, use_global_device_ids=true | all-gather | bytes 122880 | tf_op jit(solution)/shard_map/all_gather | solution.py:562
  32.0 2.8 %direction.2 = (f32[18,128,128]{2,1,0:T(8,128)S(1)}, f32[32,2,128]{2,1,0:T(2,128)S(1)}) custom-call(s32[4,32]{1,0:T(4,128)S(1)} %bitcast.19, f32[14,128,128]{2,1,0:T(8,128)S(1)} %get-tuple-element.67.refs_1_, f32[4,128,128]{2,1,0:T(8,128)S(1)} %get-tuple-element.72.refs_2_, f32[16,128,128]{2,1,0:T(8,128)S(1)} %get-tuple-element.56.refs_2__0_.refs_1__0_.refs_3__0_, ...), custom_call_target="tpu_custom_call" | custom-call | flops 400000000 | bytes 12000000 | tf_op jit(solution)/shard_map/direction/pallas_call | solution.py:446
  34.8 14.0 %all_to_all.10.refs_2_ = f32[32,2,128]{2,1,0:T(2,128)S(1)} all-to-all(f32[32,2,128]{2,1,0:T(2,128)S(1)} %get-tuple-element.75), channel_id=1, replica_groups=mesh['tm'=4,'tile'=8] {'tile','tm'}, dimensions={0} | all-to-all | bytes 65536 | tf_op jit(solution)/shard_map/all_to_all | solution.py:572
  48.8 0.7 update.1
  49.5 5.2 %all-gather.2 = f32[96,128]{1,0:T(8,128)S(1)} all-gather(f32[24,128]{1,0:T(8,128)S(1)} %get-tuple-element.79), channel_id=4, replica_groups=mesh['tm'=4,'tile'=8] {'tm'}, dimensions={0}, use_global_device_ids=true | all-gather | bytes 61440 | tf_op jit(solution)/shard_map/all_gather | solution.py:591
  54.8 2.7 %edge.3 = (bf16[2304,128]{1,0:T(8,128)(2,1)S(1)}, f32[4,128,128]{2,1,0:T(8,128)S(1)}, f32[4,128,128]{2,1,0:T(8,128)S(1)}, bf16[2,128,128]{2,1,0:T(8,128)(2,1)S(1...) custom-call(s32[4,32]{1,0:T(4,128)S(1)} %bitcast.20, f32[16,128,128]{2,1,0:T(8,128)S(1)} %get-tuple-element.77.refs_1__0_, ...), custom_call_target="tpu_custom_call" | custom-call | flops 250000000 | bytes 7500000 | tf_op jit(solution)/shard_map/edge/pallas_call | solution.py:446
  57.5 0.6 collective-permute-start.4
  58.1 0.8 collective-permute-start.5
  59.0 3.3 %inner.3 = (f32[14,128,128]{2,1,0:T(8,128)S(1)}, f32[2,24,128]{2,1,0:T(8,128)S(1)}) custom-call(s32[4,32]{1,0:T(4,128)S(1)} %bitcast.21, f32[16,128,128]{2,1,0:T(8,128)S(1)} %get-tuple-element.56.refs_2__0_.refs_1__0_.refs_3__0_, f32[2,128,128]{2,1,0:T(8,128)S(1)} %get-tuple-element.57.refs_2__1_.refs_1__1_.refs_3__1_, ...), custom_call_target="tpu_custom_call" | custom-call | flops 400000000 | bytes 12000000 | tf_op jit(solution)/shard_map/inner/pallas_call | solution.py:446
  62.3 0.0 collective-permute-done.4.refs_1_
  62.3 0.0 collective-permute-done.5.refs_2_
  62.3 0.3 border.3
  62.6 5.3 %all-gather.3 = f32[8,24,128]{2,1,0:T(8,128)S(1)} all-gather(f32[2,24,128]{2,1,0:T(8,128)S(1)} %get-tuple-element.88), channel_id=5, replica_groups=mesh['tm'=4,'tile'=8] {'tm'}, dimensions={0}, use_global_device_ids=true | all-gather | bytes 122880 | tf_op jit(solution)/shard_map/all_gather | solution.py:562
  67.9 2.8 %direction.3 = (f32[18,128,128]{2,1,0:T(8,128)S(1)}, f32[32,2,128]{2,1,0:T(2,128)S(1)}) custom-call(s32[4,32]{1,0:T(4,128)S(1)} %bitcast.22, f32[14,128,128]{2,1,0:T(8,128)S(1)} %get-tuple-element.82.refs_1_, f32[4,128,128]{2,1,0:T(8,128)S(1)} %get-tuple-element.87.refs_2_, f32[16,128,128]{2,1,0:T(8,128)S(1)} %get-tuple-element.56.refs_2__0_.refs_1__0_.refs_3__0_, ...), custom_call_target="tpu_custom_call" | custom-call | flops 400000000 | bytes 12000000 | tf_op jit(solution)/shard_map/direction/pallas_call | solution.py:446
  70.7 11.8 %all_to_all.11.refs_2_ = f32[32,2,128]{2,1,0:T(2,128)S(1)} all-to-all(f32[32,2,128]{2,1,0:T(2,128)S(1)} %get-tuple-element.90), channel_id=1, replica_groups=mesh['tm'=4,'tile'=8] {'tile','tm'}, dimensions={0} | all-to-all | bytes 65536 | tf_op jit(solution)/shard_map/all_to_all | solution.py:572
  82.5 1.3 %final.1 = f32[2048,128]{1,0:T(8,128)} custom-call(f32[16,128,128]{2,1,0:T(8,128)S(1)} %get-tuple-element.76.refs_8__0_.refs_7__0_.refs_9__0_.refs_0_, f32[18,128,128]{2,1,0:T(8,128)S(1)} %get-tuple-element.89.refs_1_, f32[32,2,128]{2,1,0:T(2,128)S(1)} %all_to_all.11.refs_2_), custom_call_target="tpu_custom_call" | custom-call | flops 140000000 | bytes 4200000 | tf_op jit(solution)/shard_map/final/pallas_call | solution.py:446
  (1 shorter events, 0.0 us)
Async XLA Ops:
  0.6 0.7 copy-start.2
  2.7 7.8 %collective-permute-start = (f32[136,128]{1,0:T(8,128)S(1)}, f32[136,128]{1,0:T(8,128)S(1)}, u32[]{:S(2)}, u32[]{:S(2)}) collective-permute-start(f32[136,128]{1,0:T(8,128)S(1)} %get-tuple-element.50), channel_id=1, source_target_pairs={{0,1},{2,3},{4,5},{6,7},{1,0},{3,2},{5,4},{7,6},{8,9},{10,11},{12,... | collective-permute-start | bytes 208904 | tf_op jit(solution)/shard_map/ppermute | solution.py:470
  5.7 4.8 %collective-permute-start.1 = (f32[136,128]{1,0:T(8,128)S(1)}, f32[136,128]{1,0:T(8,128)S(1)}, u32[]{:S(2)}, u32[]{:S(2)}) collective-permute-start(f32[136,128]{1,0:T(8,128)S(1)} %get-tuple-element.51), channel_id=1, source_target_pairs={{1,2},{3,4},{5,6},{2,1},{4,3},{6,5},{9,10},{11,12},{13,14},{10,9},... | collective-permute-start | bytes 208904 | tf_op jit(solution)/shard_map/ppermute | solution.py:470
  6.4 0.7 copy-start.3
  7.0 9.1 %copy-start = (bf16[8192,128]{1,0:T(8,128)(2,1)S(1)}, bf16[8192,128]{1,0:T(8,128)(2,1)}, u32[]{:S(2)}) copy-start(bf16[8192,128]{1,0:T(8,128)(2,1)} %refs_7_.7) | copy-start | bytes 6291460
  7.0 9.1 %copy-start.1 = (s32[32,4]{0,1:T(4,128)S(1)}, s32[32,4]{0,1:T(4,128)}, u32[]{:S(2)}) copy-start(s32[32,4]{0,1:T(4,128)} %param.8) | copy-start | bytes 1540
  18.1 8.3 %collective-permute-start.2 = (bf16[2,128,128]{2,1,0:T(8,128)(2,1)S(1)}, bf16[2,128,128]{2,1,0:T(8,128)(2,1)S(1)}, u32[]{:S(2)}, u32[]{:S(2)}) collective-permute-start(bf16[2,128,128]{2,1,0:T(8,128)(2,1)S(1)} %get-tuple-element.69), channel_id=1, source_target_pairs={{0,1},{2,3},{4,5},{6,7},{1,0},{3,2},{5,4},{7,6},{8,9},{10,11},{12,... | collective-permute-start | bytes 196616 | tf_op jit(solution)/shard_map/ppermute | solution.py:470
  22.4 4.0 %collective-permute-start.3 = (bf16[2,128,128]{2,1,0:T(8,128)(2,1)S(1)}, bf16[2,128,128]{2,1,0:T(8,128)(2,1)S(1)}, u32[]{:S(2)}, u32[]{:S(2)}) collective-permute-start(bf16[2,128,128]{2,1,0:T(8,128)(2,1)S(1)} %get-tuple-element.70), channel_id=1, source_target_pairs={{1,2},{3,4},{5,6},{2,1},{4,3},{6,5},{9,10},{11,12},{13,14},{10,9},... | collective-permute-start | bytes 196616 | tf_op jit(solution)/shard_map/ppermute | solution.py:470
  57.5 4.8 %collective-permute-start.4 = (bf16[2,128,128]{2,1,0:T(8,128)(2,1)S(1)}, bf16[2,128,128]{2,1,0:T(8,128)(2,1)S(1)}, u32[]{:S(2)}, u32[]{:S(2)}) collective-permute-start(bf16[2,128,128]{2,1,0:T(8,128)(2,1)S(1)} %get-tuple-element.84), channel_id=1, source_target_pairs={{0,1},{2,3},{4,5},{6,7},{1,0},{3,2},{5,4},{7,6},{8,9},{10,11},{12,... | collective-permute-start | bytes 196616 | tf_op jit(solution)/shard_map/ppermute | solution.py:470
  58.1 4.2 %collective-permute-start.5 = (bf16[2,128,128]{2,1,0:T(8,128)(2,1)S(1)}, bf16[2,128,128]{2,1,0:T(8,128)(2,1)S(1)}, u32[]{:S(2)}, u32[]{:S(2)}) collective-permute-start(bf16[2,128,128]{2,1,0:T(8,128)(2,1)S(1)} %get-tuple-element.85), channel_id=1, source_target_pairs={{1,2},{3,4},{5,6},{2,1},{4,3},{6,5},{9,10},{11,12},{13,14},{10,9},... | collective-permute-start | bytes 196616 | tf_op jit(solution)/shard_map/ppermute | solution.py:470

commit v2 on v1

--- a/solution.py
+++ b/solution.py
@@ -240,19 +240,21 @@
     return feet[q * PIX_BLOCK : (q + 1) * PIX_BLOCK, :]
 
 
-def pull_back(pattern, ext, feet, record, contrib, place, start, stop):
+def note_places(pattern, place, start, stop):
     for q in range(start, stop):
         for v in range(2 * HB + 1):
             place[q, v] = -1
         for k in range(K):
             place[q, pattern[k, q] - q] = k
-    for q in range(start, stop):
-        foot = foot_of(feet, q)
-        fitted = jnp.dot(foot, picked(ext, pattern, q), preferred_element_type=F32)
-        residual = (fitted - foot_of(record, q).astype(F32)).astype(BF16)
-        contrib[q * K * NEU_BLOCK : (q + 1) * K * NEU_BLOCK, :] = lax.dot_general(
-            foot, residual, (((0,), (0,)), ((), ())), preferred_element_type=F32
-        )
+
+
+def pull_back(pattern, ext, feet, record, contrib, q):
+    foot = foot_of(feet, q)
+    fitted = jnp.dot(foot, picked(ext, pattern, q), preferred_element_type=F32)
+    residual = (fitted - foot_of(record, q).astype(F32)).astype(BF16)
+    contrib[q * K * NEU_BLOCK : (q + 1) * K * NEU_BLOCK, :] = lax.dot_general(
+        foot, residual, (((0,), (0,)), ((), ())), preferred_element_type=F32
+    )
 
 
 def gathered(contrib, place, c, ranges):
@@ -277,12 +279,7 @@
 def edge_kernel(
     pattern, z3, p3, rows, pay, pays, feet, record, ext, zones, spill, send_a, send_b, *rest
 ):
-    if len(rest) > 2:
-        traces, contrib, place, traces_here, sems = rest
-    else:
-        contrib, place = rest
-        traces = None
-    copies = []
+    *traces, contrib, place = rest
     chunks = chunk_count(z3)
     stripe = pattern.shape[1]
     edge = 2 * HB
@@ -292,22 +289,24 @@
     for m in range(pays.shape[0]):
         carry = jnp.where(m < me, pays[m] + totals[m] * carry, carry)
     carry = carry * rows[1]
-    for c in range(chunks):
+    ranges = ((0, edge), (stripe - edge, stripe))
+    for start, stop in ranges:
+        note_places(pattern, place, start, stop)
+
+    def trace(c):
         field = (chunk(p3, c)[...] * (chunk(z3, c)[...] + carry[c : c + 1, :])).T
         ext[c * LANES : (c + 1) * LANES, :] = field.astype(BF16)
-        if traces is not None and RIM <= c < chunks - RIM:
-            part = (chunks - 2 * RIM) // PARTS
-            i = c - RIM
-            traces_here[i * LANES : (i + 1) * LANES, :] = field
-            if (i + 1) % part == 0:
-                at = pl.ds((i + 1 - part) * LANES, part * LANES)
-                copies.append(
-                    pltpu.make_async_copy(traces_here.at[at], traces.at[at], sems.at[i // part])
-                )
-                copies[-1].start()
-    ranges = ((0, edge), (stripe - edge, stripe))
+        if traces and RIM <= c < chunks - RIM:
+            traces[0][(c - RIM) * LANES : (c - RIM + 1) * LANES, :] = field
+
+    near = 4 * RIM
+    for c in [*range(near), *range(chunks - near, chunks)]:
+        trace(c)
     for start, stop in ranges:
-        pull_back(pattern, ext, feet, record, contrib, place, start, stop)
+        for q in range(start, stop):
+            pull_back(pattern, ext, feet, record, contrib, q)
+    for c in range(near, chunks - near):
+        trace(c)
     even = lax.axis_index("tile") % 2 == 0
     for i in range(2 * RIM):
         below = gathered(contrib, place, i, ranges)
@@ -318,8 +317,6 @@
         send_b[i] = jnp.where(even, below, above).astype(BF16)
         spill[i] = gathered(contrib, place, 2 * RIM + i, ranges)
         spill[2 * RIM + i] = gathered(contrib, place, chunks - 4 * RIM + i, ranges)
-    for copy in copies:
-        copy.wait()
 
 
 def adjoint_chunk(sums_table, field, p, pinv, rows, c, r3, pay):
@@ -332,18 +329,28 @@
     pay[1, c : c + 1, :] = ends * jnp.sum(pinv * pinv * r, axis=0, keepdims=True)
 
 
-def inner_kernel(pattern, p3, pinv3, rows, ext, spill, feet, record, r3, pay, *scratch):
-    contrib, place = scratch
+def inner_kernel(pattern, p3, pinv3, rows, ext, spill, feet, record, traces, r3, pay, *rest):
+    if traces:
+        out, contrib, place, sem = rest
+        copy = pltpu.make_async_copy(traces[0], out, sem)
+        copy.start()
+    else:
+        contrib, place = rest
     chunks = chunk_count(p3)
     frames = spill.shape[1]
     stripe = pattern.shape[1]
     edge = 2 * HB
-    pull_back(pattern, ext, feet, record, contrib, place, edge, stripe - edge)
+    per_chunk = LANES // NEU_BLOCK
+    note_places(pattern, place, edge, stripe - edge)
     sums_table = table(frames, True)
     pay[...] = jnp.zeros_like(pay)
     inner = chunks - 4 * RIM
+    q = edge
     for i in range(inner):
         c = i + 2 * RIM
+        while q < min((c + 1) * per_chunk, stripe - edge):
+            pull_back(pattern, ext, feet, record, contrib, q)
+            q += 1
         field = gathered(contrib, place, c, ((edge, stripe - edge),))
         if i < 2 * RIM:
             field = field + spill[i]
@@ -351,6 +358,8 @@
             field = field + spill[i - inner + 4 * RIM]
         p, pinv = chunk(p3, c)[...], chunk(pinv3, c)[...]
         adjoint_chunk(sums_table, field, p, pinv, rows, c, r3.at[i], pay)
+    if traces:
+        copy.wait()
 
 
 def border_kernel(zones, got_a, got_b, p3, pinv3, rows, pay_inner, r3, pay):
@@ -391,6 +400,9 @@
     carry = carry * rows[1]
     sums_table = table(frames, False)
     grad_sq = jnp.zeros((8, LANES), F32)
+    image_sq = jnp.zeros((8, frames), F32)
+    per_chunk = LANES // NEU_BLOCK
+    q = 0
     for c in range(chunks):
         p, pinv = chunk(p3, c)[...], chunk(pinv3, c)[...]
         if c < 2 * RIM:
@@ -407,10 +419,10 @@
         z = summed(sums_table, gain * gradient * pinv)
         field = (p * (z + carry[c : c + 1, :])).T
         ext[c * LANES : (c + 1) * LANES, :] = field.astype(BF16)
-    image_sq = jnp.zeros((8, frames), F32)
-    for q in range(stripe):
-        image = jnp.dot(foot_of(feet, q), picked(ext, pattern, q), preferred_element_type=F32)
-        image_sq += jnp.sum((image * image).reshape(PIX_BLOCK // 8, 8, frames), axis=0)
+        while q < stripe and q + 2 * HB < (c + 1) * per_chunk:
+            image = jnp.dot(foot_of(feet, q), picked(ext, pattern, q), preferred_element_type=F32)
+            image_sq += jnp.sum((image * image).reshape(PIX_BLOCK // 8, 8, frames), axis=0)
+            q += 1
     both = jnp.concatenate(
         [
             jnp.sum(grad_sq, axis=0, keepdims=True),
@@ -536,19 +548,20 @@
             )
             + ((f32(neurons, frames),) if ends else ()),
             (pattern, z3, p3, rows, constants, pays, footprints, recording),
-            scratch + (staged if ends else []),
-            far_out=(5,),
+            scratch,
             keep=(s3[0],) if ends else (),
         )
         got_a, got_b = swapped(send_a, send_b)
         held = (s3[0],) if ends else ()
-        r_inner, pay = call(
+        r_inner, pay, *traces = call(
             inner_kernel,
             "inner",
             4.0,
-            (f32(chunks - 4 * RIM, frames, LANES), f32(2, lines, LANES)),
-            (pattern, p3, pinv3, rows, ext, spill, footprints, recording),
-            scratch,
+            (f32(chunks - 4 * RIM, frames, LANES), f32(2, lines, LANES))
+            + ((f32(neurons, frames),) if ends else ()),
+            (pattern, p3, pinv3, rows, ext, spill, footprints, recording, traces),
+            scratch + ([pltpu.SemaphoreType.DMA] if ends else []),
+            far_out=(2,),
             keep=held,
         )
         r_border, pay = call(

time: 84.3 us -> 95.2 us (1.13)
  Pallas kernels: 24.4 us -> 35.9 us
    pallas_call x13, Pallas kernels: 24.4 us -> 35.9 us  [call(): pl.pallas_call(body, name=name, out_shape=outs, in_specs=in_specs, out_sp...]
  transfers between devices with their start and end apart: 6 -> 6, of which waited for: 0 -> 0; matrix products, arithmetic and copies ran while one was open for 0% -> 0% of each run, Pallas kernels for 12% -> 17%
where the time goes in v2:
time: 95.2 us; the launch traced here: 94.9 us
  blocking collectives  46.7 us (49%)
  Pallas kernels  35.9 us (38%)
  starting transfers between devices  9.97 us (10%)
  local copies, waits for them, and re-layouts  1.35 us (1%)
  between operations  0.97 us (1%)
    pallas_call x13, Pallas kernels, call(): pl.pallas_call(body, name=name, out_shape=outs, in_specs=in_specs, out_sp...  35.9 us
    all_to_all x2, blocking collectives, per_device(): stats = lax.all_to_all(stats, ('tile', 'tm'), 0, 0)  25.3 us
    all_gather x3, blocking collectives, per_device(): pays = lax.all_gather(pay, 'tm')  16.1 us
    ppermute x3, starting transfers between devices, swapped(): lax.ppermute(first, 'tile', pairs(0))  8.01 us
    all_gather x1, blocking collectives, per_device(): constants = lax.all_gather(pay, 'tm')  5.34 us
    ppermute x3, starting transfers between devices, swapped(): lax.ppermute(second, 'tile', pairs(1))  1.96 us
  transfers between devices with their start and end apart: 6, of which 0 were waited for; matrix products, arithmetic and copies ran while one was open for 0% of the time, Pallas kernels for 17%

profile of v2, /device:TPU:0, one launch (start us, length us, event | category | flops | bytes accessed | tf_op | source)
XLA Modules:
  0.0 94.9 jit_solution(11576615128313433621)
XLA Ops:
  0.6 0.0 copy-start.2
  0.6 0.7 copy-done.2
  1.3 1.4 %rims.1 = (f32[136,128]{1,0:T(8,128)S(1)}, f32[136,128]{1,0:T(8,128)S(1)}, f32[16,128]{1,0:T(8,128)S(1)}, f32[2048,128]{1,0:T(8,128)S(1)}) custom-call(f32[2048,128]{1,0:T(8,128)} %refs_0_.1, f32[16,128]{1,0:T(8,128)S(1)} %bitcast.23), custom_call_target="tpu_custom_call" | custom-call | flops 100000000 | bytes 3000000 | tf_op jit(solution)/shard_map/rims/pallas_call | solution.py:458
  2.7 3.0 %collective-permute-start = (f32[136,128]{1,0:T(8,128)S(1)}, f32[136,128]{1,0:T(8,128)S(1)}, u32[]{:S(2)}, u32[]{:S(2)}) collective-permute-start(f32[136,128]{1,0:T(8,128)S(1)} %get-tuple-element.51), channel_id=1, source_target_pairs={{0,1},{2,3},{4,5},{6,7},{1,0},{3,2},{5,4},{7,6},{8,9},{10,11},{12,... | collective-permute-start | bytes 208904 | tf_op jit(solution)/shard_map/ppermute | solution.py:482
  5.7 0.7 collective-permute-start.1
  6.4 0.0 copy-start.3
  6.4 0.6 copy-done.3
  7.0 0.0 copy-start
  7.0 0.0 copy-start.1
  7.0 3.4 %prep_own.1 = (f32[16,128,128]{2,1,0:T(8,128)S(1)}, f32[16,128,128]{2,1,0:T(8,128)S(1)}, f32[16,128,128]{2,1,0:T(8,128)S(1)}, f32[16,128,128]{2,1,0:T(8,128)S(1)...) custom-call(f32[2048,128]{1,0:T(8,128)S(1)} %get-tuple-element.48.re, ...), custom_call_target="tpu_custom_call" | custom-call | flops 160000000 | bytes 4800000 | tf_op jit(solution)/shard_map/prep_own/pallas_call | solution.py:458
  10.5 0.0 collective-permute-done.refs_0_
  10.5 0.0 collective-permute-done.1.refs_1_
  10.5 0.3 prep_rim.1
  10.8 5.3 %all-gather = f32[8,24,128]{2,1,0:T(8,128)S(1)} all-gather(f32[2,24,128]{2,1,0:T(8,128)S(1)} %get-tuple-element.64), channel_id=2, replica_groups=mesh['tm'=4,'tile'=8] {'tm'}, dimensions={0}, use_global_device_ids=true | all-gather | bytes 122880 | tf_op jit(solution)/shard_map/all_gather | solution.py:527
  16.1 0.0 copy-done
  16.1 0.0 copy-done.1
  16.1 1.9 %edge.2 = (bf16[2304,128]{1,0:T(8,128)(2,1)S(1)}, f32[4,128,128]{2,1,0:T(8,128)S(1)}, f32[4,128,128]{2,1,0:T(8,128)S(1)}, bf16[2,128,128]{2,1,0:T(8,128)(2,1)S(1)}, bf16[2,128,128]{2,1,0:T(8,128)(2,1)S(1)}) custom-call(s32[4,32]{1,0:T(4,128)S(1)} %bitcast.17, f32[16,128,128]{2,1,0:T(8,128)S(1)} %get-tuple-element.62.refs_1__0_, ...), custom_call_target="tpu_custom_call" | custom-call | flops 250000000 | bytes 7500000 | tf_op jit(solution)/shard_map/edge/pallas_call | solution.py:458
  18.0 4.3 %collective-permute-start.2 = (bf16[2,128,128]{2,1,0:T(8,128)(2,1)S(1)}, bf16[2,128,128]{2,1,0:T(8,128)(2,1)S(1)}, u32[]{:S(2)}, u32[]{:S(2)}) collective-permute-start(bf16[2,128,128]{2,1,0:T(8,128)(2,1)S(1)} %get-tuple-element.70), channel_id=1, source_target_pairs={{0,1},{2,3},{4,5},{6,7},{1,0},{3,2},{5,4},{7,6},{8,9},{10,11},{12,... | collective-permute-start | bytes 196616 | tf_op jit(solution)/shard_map/ppermute | solution.py:482
  22.4 0.7 collective-permute-start.3
  23.0 5.9 %inner.2 = (f32[14,128,128]{2,1,0:T(8,128)S(1)}, f32[2,24,128]{2,1,0:T(8,128)S(1)}) custom-call(s32[4,32]{1,0:T(4,128)S(1)} %bitcast.18, f32[16,128,128]{2,1,0:T(8,128)S(1)} %get-tuple-element.57.refs_2__0_.refs_1__0_.refs_3__0_, f32[2,128,128]{2,1,0:T(8,128)S(1)} %get-tuple-element.58.refs_2__1_.refs_1__1_.refs_3__1_, ...), custom_call_target="tpu_custom_call" | custom-call | flops 400000000 | bytes 12000000 | tf_op jit(solution)/shard_map/inner/pallas_call | solution.py:458
  28.9 0.0 collective-permute-done.2.refs_1_
  28.9 0.0 collective-permute-done.3.refs_2_
  28.9 0.3 border.2
  29.2 5.3 %all-gather.1 = f32[8,24,128]{2,1,0:T(8,128)S(1)} all-gather(f32[2,24,128]{2,1,0:T(8,128)S(1)} %get-tuple-element.74), channel_id=3, replica_groups=mesh['tm'=4,'tile'=8] {'tm'}, dimensions={0}, use_global_device_ids=true | all-gather | bytes 122880 | tf_op jit(solution)/shard_map/all_gather | solution.py:575
  34.5 6.0 %direction.2 = (f32[18,128,128]{2,1,0:T(8,128)S(1)}, f32[32,2,128]{2,1,0:T(2,128)S(1)}) custom-call(s32[4,32]{1,0:T(4,128)S(1)} %bitcast.19, f32[14,128,128]{2,1,0:T(8,128)S(1)} %get-tuple-element.68.refs_1_, f32[4,128,128]{2,1,0:T(8,128)S(1)} %get-tuple-element.73.refs_2_, f32[16,128,128]{2,1,0:T(8,128)S(1)} %get-tuple-element.57.refs_2__0_.refs_1__0_.refs_3__0_, ...), custom_call_target="tpu_custom_call" | custom-call | flops 400000000 | bytes 12000000 | tf_op jit(solution)/shard_map/direction/pallas_call | solution.py:458
  40.5 13.6 %all_to_all.10.refs_2_ = f32[32,2,128]{2,1,0:T(2,128)S(1)} all-to-all(f32[32,2,128]{2,1,0:T(2,128)S(1)} %get-tuple-element.76), channel_id=1, replica_groups=mesh['tm'=4,'tile'=8] {'tile','tm'}, dimensions={0} | all-to-all | bytes 65536 | tf_op jit(solution)/shard_map/all_to_all | solution.py:585
  54.2 0.7 update.1
  54.9 5.4 %all-gather.2 = f32[96,128]{1,0:T(8,128)S(1)} all-gather(f32[24,128]{1,0:T(8,128)S(1)} %get-tuple-element.80), channel_id=4, replica_groups=mesh['tm'=4,'tile'=8] {'tm'}, dimensions={0}, use_global_device_ids=true | all-gather | bytes 61440 | tf_op jit(solution)/shard_map/all_gather | solution.py:604
  60.3 1.9 %edge.3 = (bf16[2304,128]{1,0:T(8,128)(2,1)S(1)}, f32[4,128,128]{2,1,0:T(8,128)S(1)}, f32[4,128,128]{2,1,0:T(8,128)S(1)}, bf16[2,128,128]{2,1,0:T(8,128)(2,1)S(1...) custom-call(s32[4,32]{1,0:T(4,128)S(1)} %bitcast.20, f32[16,128,128]{2,1,0:T(8,128)S(1)} %get-tuple-element.78.refs_1__0_, ...), custom_call_target="tpu_custom_call" | custom-call | flops 250000000 | bytes 7500000 | tf_op jit(solution)/shard_map/edge/pallas_call | solution.py:458
  62.2 0.6 collective-permute-start.4
  62.9 0.7 collective-permute-start.5
  63.5 6.6 %inner.3 = (f32[14,128,128]{2,1,0:T(8,128)S(1)}, f32[2,24,128]{2,1,0:T(8,128)S(1)}, f32[2048,128]{1,0:T(8,128)}) custom-call(s32[4,32]{1,0:T(4,128)S(1)} %bitcast.21, f32[16,128,128]{2,1,0:T(8,128)S(1)} %get-tuple-element.57.refs_2__0_.refs_1__0_.refs_3__0_, f32[2,128,128]{2,1,0:T(8,128)S(1)} %get-tuple-element.58.refs_2__1_.refs_1__1_.refs_3__1_, ...), custom_call_target="tpu_custom_call" | custom-call | flops 400000000 | bytes 12000000 | tf_op jit(solution)/shard_map/inner/pallas_call | solution.py:458
  70.1 0.0 collective-permute-done.4.refs_1_
  70.1 0.0 collective-permute-done.5.refs_2_
  70.1 0.3 border.3
  70.4 5.3 %all-gather.3 = f32[8,24,128]{2,1,0:T(8,128)S(1)} all-gather(f32[2,24,128]{2,1,0:T(8,128)S(1)} %get-tuple-element.90), channel_id=5, replica_groups=mesh['tm'=4,'tile'=8] {'tm'}, dimensions={0}, use_global_device_ids=true | all-gather | bytes 122880 | tf_op jit(solution)/shard_map/all_gather | solution.py:575
  75.8 6.0 %direction.3 = (f32[18,128,128]{2,1,0:T(8,128)S(1)}, f32[32,2,128]{2,1,0:T(2,128)S(1)}) custom-call(s32[4,32]{1,0:T(4,128)S(1)} %bitcast.22, f32[14,128,128]{2,1,0:T(8,128)S(1)} %get-tuple-element.84.refs_1_, f32[4,128,128]{2,1,0:T(8,128)S(1)} %get-tuple-element.89.refs_2_, f32[16,128,128]{2,1,0:T(8,128)S(1)} %get-tuple-element.57.refs_2__0_.refs_1__0_.refs_3__0_, ...), custom_call_target="tpu_custom_call" | custom-call | flops 400000000 | bytes 12000000 | tf_op jit(solution)/shard_map/direction/pallas_call | solution.py:458
  81.8 11.7 %all_to_all.11.refs_2_ = f32[32,2,128]{2,1,0:T(2,128)S(1)} all-to-all(f32[32,2,128]{2,1,0:T(2,128)S(1)} %get-tuple-element.92), channel_id=1, replica_groups=mesh['tm'=4,'tile'=8] {'tile','tm'}, dimensions={0} | all-to-all | bytes 65536 | tf_op jit(solution)/shard_map/all_to_all | solution.py:585
  93.4 1.3 %final.1 = f32[2048,128]{1,0:T(8,128)} custom-call(f32[16,128,128]{2,1,0:T(8,128)S(1)} %get-tuple-element.77.refs_8__0_.refs_9__0_.refs_7__0_.refs_0_, f32[18,128,128]{2,1,0:T(8,128)S(1)} %get-tuple-element.91.refs_1_, f32[32,2,128]{2,1,0:T(2,128)S(1)} %all_to_all.11.refs_2_), custom_call_target="tpu_custom_call" | custom-call | flops 140000000 | bytes 4200000 | tf_op jit(solution)/shard_map/final/pallas_call | solution.py:458
  (1 shorter events, 0.0 us)
Async XLA Ops:
  0.6 0.7 copy-start.2
  2.7 7.8 %collective-permute-start = (f32[136,128]{1,0:T(8,128)S(1)}, f32[136,128]{1,0:T(8,128)S(1)}, u32[]{:S(2)}, u32[]{:S(2)}) collective-permute-start(f32[136,128]{1,0:T(8,128)S(1)} %get-tuple-element.51), channel_id=1, source_target_pairs={{0,1},{2,3},{4,5},{6,7},{1,0},{3,2},{5,4},{7,6},{8,9},{10,11},{12,... | collective-permute-start | bytes 208904 | tf_op jit(solution)/shard_map/ppermute | solution.py:482
  5.7 4.8 %collective-permute-start.1 = (f32[136,128]{1,0:T(8,128)S(1)}, f32[136,128]{1,0:T(8,128)S(1)}, u32[]{:S(2)}, u32[]{:S(2)}) collective-permute-start(f32[136,128]{1,0:T(8,128)S(1)} %get-tuple-element.52), channel_id=1, source_target_pairs={{1,2},{3,4},{5,6},{2,1},{4,3},{6,5},{9,10},{11,12},{13,14},{10,9},... | collective-permute-start | bytes 208904 | tf_op jit(solution)/shard_map/ppermute | solution.py:482
  6.4 0.7 copy-start.3
  7.0 9.1 %copy-start = (bf16[8192,128]{1,0:T(8,128)(2,1)S(1)}, bf16[8192,128]{1,0:T(8,128)(2,1)}, u32[]{:S(2)}) copy-start(bf16[8192,128]{1,0:T(8,128)(2,1)} %refs_7_.7) | copy-start | bytes 6291460
  7.0 9.1 %copy-start.1 = (s32[32,4]{0,1:T(4,128)S(1)}, s32[32,4]{0,1:T(4,128)}, u32[]{:S(2)}) copy-start(s32[32,4]{0,1:T(4,128)} %param.8) | copy-start | bytes 1540
  18.0 10.9 %collective-permute-start.2 = (bf16[2,128,128]{2,1,0:T(8,128)(2,1)S(1)}, bf16[2,128,128]{2,1,0:T(8,128)(2,1)S(1)}, u32[]{:S(2)}, u32[]{:S(2)}) collective-permute-start(bf16[2,128,128]{2,1,0:T(8,128)(2,1)S(1)} %get-tuple-element.70), channel_id=1, source_target_pairs={{0,1},{2,3},{4,5},{6,7},{1,0},{3,2},{5,4},{7,6},{8,9},{10,11},{12,... | collective-permute-start | bytes 196616 | tf_op jit(solution)/shard_map/ppermute | solution.py:482
  22.4 6.6 %collective-permute-start.3 = (bf16[2,128,128]{2,1,0:T(8,128)(2,1)S(1)}, bf16[2,128,128]{2,1,0:T(8,128)(2,1)S(1)}, u32[]{:S(2)}, u32[]{:S(2)}) collective-permute-start(bf16[2,128,128]{2,1,0:T(8,128)(2,1)S(1)} %get-tuple-element.71), channel_id=1, source_target_pairs={{1,2},{3,4},{5,6},{2,1},{4,3},{6,5},{9,10},{11,12},{13,14},{10,9},... | collective-permute-start | bytes 196616 | tf_op jit(solution)/shard_map/ppermute | solution.py:482
  62.2 7.9 %collective-permute-start.4 = (bf16[2,128,128]{2,1,0:T(8,128)(2,1)S(1)}, bf16[2,128,128]{2,1,0:T(8,128)(2,1)S(1)}, u32[]{:S(2)}, u32[]{:S(2)}) collective-permute-start(bf16[2,128,128]{2,1,0:T(8,128)(2,1)S(1)} %get-tuple-element.86), channel_id=1, source_target_pairs={{0,1},{2,3},{4,5},{6,7},{1,0},{3,2},{5,4},{7,6},{8,9},{10,11},{12,... | collective-permute-start | bytes 196616 | tf_op jit(solution)/shard_map/ppermute | solution.py:482
  62.9 7.3 %collective-permute-start.5 = (bf16[2,128,128]{2,1,0:T(8,128)(2,1)S(1)}, bf16[2,128,128]{2,1,0:T(8,128)(2,1)S(1)}, u32[]{:S(2)}, u32[]{:S(2)}) collective-permute-start(bf16[2,128,128]{2,1,0:T(8,128)(2,1)S(1)} %get-tuple-element.87), channel_id=1, source_target_pairs={{1,2},{3,4},{5,6},{2,1},{4,3},{6,5},{9,10},{11,12},{13,14},{10,9},... | collective-permute-start | bytes 196616 | tf_op jit(solution)/shard_map/ppermute | solution.py:482
